TPU v7x, 256 devices: a whole 4x4x8 slice. The times are simulated.
256 devices in a mesh: blk: 16 (over z, x_hi), slab: 16 (over x_lo, y, core).
Axes of the slice: x: 4 (x_hi: 2, x_lo: 2; x = x_hi * 2 + x_lo), y: 4, z: 8, core: 2. Of those that a mesh axis runs over, the one named last changes fastest.
Arguments:
- orbitals: float32 [64, 48, 48, 240], P('blk', 'slab'), may hold values from -7 to 7
- kernel: float32 [48, 48, 240], replicated, may hold values from 0.02 to 25, as said below
Outputs:
- exchange_terms: float32 [64, 48, 48, 240], P('blk', 'slab')
- margin: float32 [64, 64], P(None, 'blk')
Inputs may be any that keep to these rules, and one draw needn't show every extreme that they name: kernel is positive and even in each frequency index: kernel[a, b, c] equals kernel[(48 - a) mod 48, b, c], kernel[a, (48 - b) mod 48, c] and kernel[a, b, (240 - c) mod 240].
All inputs are finite; a program needn't handle non-finite values.
Results may differ from a plain program's by a relative error of at most 0.0003.
Values sent between devices are 32-bit elements; how exact they have to be, the bound alone decides.
No kernel may reach another device: no remote copies, remote signals or barrier semaphores. Data moves between devices by JAX's collectives and lax.ppermute only.
A program may use at most 128 MiB of HBM per device.

v0:
```python
import functools
import math

import jax
import jax.numpy as jnp
import ml_dtypes
import numpy as np
from jax import lax
from jax.experimental import pallas as pl
from jax.experimental.pallas import tpu as pltpu
from jax.sharding import Mesh, PartitionSpec as P

NX = 48
NY = 48
NZ = 240
LANES = 256
EVEN = 26
ODD = 24
GRID = NX * NY * NZ

bf16 = jnp.bfloat16
f32 = jnp.float32
highest = lax.Precision.HIGHEST


def halves(table):
    high = table.astype(ml_dtypes.bfloat16)
    low = (table - high.astype(np.float64)).astype(ml_dtypes.bfloat16)
    return high, low


def cas(length):
    position = np.arange(length)
    angles = (position[:, None] * position[None, :] % length) * (2.0 * math.pi / length)
    return np.cos(angles) + np.sin(angles)


def left_table(table):
    high, low = halves(table)
    return np.concatenate([high, low, high], axis=1)


WIDTH = 3 * LANES
ROWS = (LANES, 192, 8 * EVEN, 8 * ODD, 8 * EVEN, 8 * ODD)
FIRST = tuple(sum(ROWS[:k]) for k in range(len(ROWS) + 1))


def make_table():
    table_z = np.zeros((LANES, LANES))
    table_z[:NZ, :NZ] = cas(NZ)
    high, low = halves(table_z)
    along_z = np.concatenate([high, high, low], axis=1)
    along_y = left_table(np.kron(np.eye(4), cas(NY)))
    place = np.arange(NX // 2 + 1)
    angles = (place[:, None] * place[None, :] % NX) * (2.0 * math.pi / NX)
    even = np.zeros((EVEN, EVEN))
    even[:25, :25] = np.cos(angles)
    odd = np.zeros((ODD, ODD))
    odd[:24, :24] = np.sin(angles)[:24, :24]
    weight = np.full(EVEN, 2.0)
    weight[0] = weight[24] = 1.0
    eye = np.eye(8)
    even_there = left_table(np.kron(even, eye))
    odd_there = left_table(np.kron(odd, eye))
    even_back = left_table(np.kron(even * weight[None, :] * (-1.0 / GRID), eye))
    odd_back = left_table(np.kron(odd * (-2.0 / GRID), eye))
    table = np.zeros((FIRST[-1], WIDTH), ml_dtypes.bfloat16)
    parts = (along_z, along_y, even_there, odd_there, even_back, odd_back)
    for first, part in zip(FIRST, parts):
        table[first : first + part.shape[0], : part.shape[1]] = part
    return table


def split(value):
    high = value.astype(bf16)
    low = (value - high.astype(f32)).astype(bf16)
    return high, low


def from_right(rows, table):
    high, low = split(rows)
    result = jnp.dot(high, table[0:LANES, 0:LANES], preferred_element_type=f32)
    result += jnp.dot(low, table[0:LANES, LANES : 2 * LANES], preferred_element_type=f32)
    return result + jnp.dot(high, table[0:LANES, 2 * LANES :], preferred_element_type=f32)


def from_left(table, k, rows):
    high, low = split(rows)
    stacked = jnp.concatenate([high, high, low], axis=0)
    return jnp.dot(
        table[FIRST[k] : FIRST[k + 1], : stacked.shape[0]], stacked, preferred_element_type=f32
    )


def widen(value):
    return jnp.pad(value, [(0, 0)] * (value.ndim - 1) + [(0, LANES - NZ)])


def pair_kernel(count, last, *refs):
    refs = list(refs)
    place, table_hbm, filt_hbm = refs[:3]
    target_parts, refs = refs[3:8], refs[8:]
    field_parts, refs = [refs[4 * s : 4 * s + 4] for s in range(count)], refs[4 * count :]
    if last:
        carried, up_first, down_first, up_second, down_second, keep = refs[:6]
        refs = refs[6:]
    else:
        out, refs = refs[0], refs[1:]
    targets, sources, source, product, planes, total, table, filt, sems = refs
    xl, y, core = place[0], place[1], place[2]

    part, lower, low_far, high_far, upper = target_parts
    table_copy = pltpu.make_async_copy(table_hbm, table, sems.at[3])
    filt_copy = pltpu.make_async_copy(filt_hbm.at[pl.ds(0, EVEN)], filt, sems.at[4])
    target_copies = [
        pltpu.make_async_copy(ref, dst, sems.at[5])
        for ref, dst in (
            (part, targets.at[0]),
            (lower, targets.at[1]),
            (low_far, targets.at[2, 0]),
            (high_far, targets.at[2, 1]),
            (upper, targets.at[3]),
        )
    ]
    source_copies = [
        pltpu.make_async_copy(ref, sources.at[s, q], sems.at[s])
        for s, parts in enumerate(field_parts)
        for q, ref in enumerate(parts)
    ]
    carry_copies = [pltpu.make_async_copy(carried, total, sems.at[2])] if last else []
    for copy in target_copies + source_copies[:4] + [table_copy, filt_copy] + source_copies[4:] + carry_copies:
        copy.start()

    def base(i, r, j):
        return (xl ^ i) * 24 + ((y + r) % 4) * 6 + (core ^ j) * 3

    pieces = [(r, i, j) for r in range(4) for i in range(2) for j in range(2)]
    planes[25] = jnp.zeros((NY, LANES), f32)
    planes[EVEN] = jnp.zeros((NY, LANES), f32)
    for copy in target_copies:
        copy.wait()

    def members(k):
        if k < 11:
            a = 2 * k + 1
            return (a, a + 1, EVEN + a, EVEN + a + 1)
        return (0, 24, 23, EVEN + 23)

    def products(s):
        for r, i, j in pieces:
            start = base(i, 4 - r, j)
            values = sources[s, 2 * i + j, r]
            source[pl.ds(start, 3)] = values
            product[pl.ds(start, 3)] = values * targets[r, i, j]

    def visit(s):
        for k in range(12):
            if k < 11:
                a = 2 * k + 1
                fa, ga, fb, gb = (product[x] for x in (a, NX - a, a + 1, NX - a - 1))
                rows = [fa + ga, fb + gb, fa - ga, fb - gb]
            else:
                fa, ga = product[23], product[25]
                rows = [product[0], product[24], fa + ga, fa - ga]
            rows = widen(jnp.concatenate(rows, axis=0))
            rows = from_right(rows, table)
            rows = from_left(table, 1, rows).reshape(4, NY, LANES)
            for m, plane in enumerate(members(k)):
                planes[plane] = rows[m]

        for t in range(6):
            band = pl.ds(8 * t, 8)
            screen = widen(filt[0:EVEN, band, :])
            for there, back, lo, size in ((2, 4, 0, EVEN), (3, 5, EVEN, ODD)):
                rows = planes[lo : lo + size, band, :].reshape(size * 8, LANES)
                rows = from_left(table, there, rows)
                rows = rows * screen[:size].reshape(size * 8, LANES)
                rows = from_left(table, back, rows)
                planes[lo : lo + size, band, :] = rows.reshape(size, 8, LANES)

        def add(x, value):
            value = value[:, :NZ] * source[x]
            total[x] = total[x] + value if last else value

        for k in range(12):
            rows = jnp.concatenate([planes[plane] for plane in members(k)], axis=0)
            rows = from_left(table, 1, rows)
            rows = from_right(rows, table).reshape(4, NY, LANES)
            if k < 11:
                a = 2 * k + 1
                for m in range(2):
                    add(a + m, rows[m] + rows[m + 2])
                    add(NX - a - m, rows[m] - rows[m + 2])
            else:
                add(0, rows[0])
                add(24, rows[1])
                add(23, rows[2] + rows[3])
                add(25, rows[2] - rows[3])

    if count == 1:
        for copy in source_copies:
            copy.wait()
        products(0)
        table_copy.wait()
        filt_copy.wait()
        visit(0)
    else:

        @pl.loop(0, count)
        def _(s):
            for q in range(4):
                pltpu.make_async_copy(sources.at[s, q], sources.at[s, q], sems.at[s]).wait()

            @pl.when(s == 0)
            def _():
                table_copy.wait()
                filt_copy.wait()
                for copy in carry_copies:
                    copy.wait()

            products(s)
            visit(s)

    if last:
        homes = {
            (0, 0): keep.at[0], (0, 1): keep.at[1],
            (1, 0): up_second, (1, 1): up_first.at[1],
            (2, 0): up_first.at[0], (2, 1): down_first.at[0],
            (3, 0): down_first.at[1], (3, 1): down_second,
        }
        copies = [
            pltpu.make_async_copy(total.at[pl.ds(base(i, r, j), 3)], homes[r, i].at[j], sems.at[5])
            for r, i, j in pieces
        ]
    else:
        copies = [pltpu.make_async_copy(total, out, sems.at[5])]
    for copy in copies:
        copy.start()
    for copy in copies:
        copy.wait()


def pair_terms(place, target_parts, fields, kernel, table, carried):
    count, last = len(fields), carried is not None
    operands = [place, table, kernel, *target_parts, *[part for field in fields for part in field]]
    whole = jax.ShapeDtypeStruct((2, 2, 3, NY, NZ), f32)
    piece = jax.ShapeDtypeStruct((2, 3, NY, NZ), f32)
    hbm = pl.BlockSpec(memory_space=pl.ANY)
    if last:
        operands.append(carried)
        out_shape, out_specs = [whole, whole, piece, piece, whole], [hbm] * 5
    else:
        out_shape, out_specs = jax.ShapeDtypeStruct((NX, NY, NZ), f32), hbm
    return pl.pallas_call(
        functools.partial(pair_kernel, count, last),
        out_shape=out_shape,
        in_specs=[pl.BlockSpec(memory_space=pltpu.SMEM)] + [hbm] * (len(operands) - 1),
        out_specs=out_specs,
        scratch_shapes=[
            pltpu.VMEM((4, 2, 2, 3, NY, NZ), f32),
            pltpu.VMEM((count, 4, 4, 3, NY, NZ), f32),
            pltpu.VMEM((NX, NY, NZ), f32),
            pltpu.VMEM((NX, NY, NZ), f32),
            pltpu.VMEM((EVEN + ODD, NY, LANES), f32),
            pltpu.VMEM((NX, NY, NZ), f32),
            pltpu.VMEM((FIRST[-1], WIDTH), bf16),
            pltpu.VMEM((EVEN, NY, NZ), f32),
            pltpu.SemaphoreType.DMA((6,)),
        ],
        compiler_params=pltpu.CompilerParams(vmem_limit_bytes=60 * 2**20),
        cost_estimate=pl.CostEstimate(flops=1000, bytes_accessed=1000, transcendentals=0),
        name="pair_terms",
    )(*operands)


def early_kernel(place, orbitals, theirs, own, own_other, near_other, far, lower, upper, stacked, both):
    xh = place[3]
    for n, part in enumerate((own, own_other, near_other, far)):
        stacked[n] = part[...]
    both[pl.ds(4 * xh, 4)] = orbitals[:, :, pl.ds(pl.multiple_of(24 * xh, 8), 24), :]
    both[pl.ds(4 * (1 - xh), 4)] = theirs[...]


def gather_early(place, orbitals, theirs, own, own_other, near_other, far, lower, upper):
    vmem = pl.BlockSpec(memory_space=pltpu.VMEM)
    hbm = pl.BlockSpec(memory_space=pl.ANY)
    return pl.pallas_call(
        early_kernel,
        out_shape=[
            jax.ShapeDtypeStruct((4,) + own.shape, f32),
            jax.ShapeDtypeStruct((8, 3, NY // 2, NZ), f32),
        ],
        in_specs=[pl.BlockSpec(memory_space=pltpu.SMEM)] + [vmem] * 6 + [hbm] * 2,
        out_specs=[vmem] * 2,
        compiler_params=pltpu.CompilerParams(vmem_limit_bytes=12 * 2**20),
        cost_estimate=pl.CostEstimate(flops=1000, bytes_accessed=1000, transcendentals=0),
        name="gather_early",
    )(place, orbitals, theirs, own, own_other, near_other, far, lower, upper)


def late_kernel(near, far_other, total, stacked):
    stacked[0] = near[...]
    stacked[1] = far_other[...]


def gather_late(near, far_other, total):
    vmem = pl.BlockSpec(memory_space=pltpu.VMEM)
    return pl.pallas_call(
        late_kernel,
        out_shape=jax.ShapeDtypeStruct((2,) + near.shape, f32),
        in_specs=[vmem] * 2 + [pl.BlockSpec(memory_space=pl.ANY)],
        out_specs=vmem,
        compiler_params=pltpu.CompilerParams(vmem_limit_bytes=8 * 2**20),
        cost_estimate=pl.CostEstimate(flops=1000, bytes_accessed=1000, transcendentals=0),
        name="gather_late",
    )(near, far_other, total)


def margin_kernel(place, terms, theirs, orbitals, out, sums):
    here = 2 * place[0] + place[2]
    xh = place[3]
    step = pl.program_id(0)

    @pl.loop(0, 8)
    def _(p):
        totals = [[None] * 8 for _ in range(2)]
        for x in range(3):
            for t in range(3):
                rows = pl.ds(8 * t, 8)
                mine = pl.ds(pl.multiple_of(xh * 24 + 8 * t, 8), 8)
                values = [orbitals[2 * p + m, x, rows, :] for m in range(2)]
                for k in range(8):
                    term = terms[k, x, mine, :] if k < 4 else theirs[(k - 4) ^ here, x, rows, :]
                    for m in range(2):
                        value = term * values[m]
                        totals[m][k] = value if totals[m][k] is None else totals[m][k] + value
        for m in range(2):
            for k in range(8):
                sums[k // 4, 2 * p + m, k % 4] = totals[m][k]

    rows = sums[...].reshape(1024, NZ) * (1.0 / GRID)
    high, low = split(rows)
    ones = jnp.ones((NZ, 128), bf16)
    rows = jnp.dot(high, ones, preferred_element_type=f32)
    rows += jnp.dot(low, ones, preferred_element_type=f32)
    rows = jnp.sum(rows.reshape(128, 8, 128), axis=1)
    place_of = lax.broadcasted_iota(jnp.int32, (128, 128), 0)
    lane_of = lax.broadcasted_iota(jnp.int32, (128, 128), 1)
    line = jnp.sum(jnp.where(place_of == lane_of, rows, 0.0), axis=0, keepdims=True)
    for g in range(2):
        row = jnp.broadcast_to(line[:, 64 * g : 64 * g + 64], (16, 64))
        out[pl.ds((xh ^ g) * 16, 16), pl.ds(step, 1), :] = row.reshape(16, 1, 64)


def margin_shares(place, terms, theirs, orbitals):
    vmem = pl.BlockSpec(memory_space=pltpu.VMEM)
    return pl.pallas_call(
        margin_kernel,
        grid=(4,),
        out_shape=jax.ShapeDtypeStruct((32, 4, 64), f32),
        in_specs=[
            pl.BlockSpec(memory_space=pltpu.SMEM),
            vmem,
            vmem,
            pl.BlockSpec((16, 3, NY // 2, NZ), lambda z: (z, 0, 0, 0)),
        ],
        out_specs=pl.BlockSpec((32, 4, 64), lambda z: (0, 0, 0)),
        scratch_shapes=[pltpu.VMEM((2, 16, 4, 8, NZ), f32)],
        compiler_params=pltpu.CompilerParams(vmem_limit_bytes=60 * 2**20),
        cost_estimate=pl.CostEstimate(flops=1000, bytes_accessed=1000, transcendentals=0),
        name="margin_shares",
    )(place, terms, theirs, orbitals)


def moved(array, axes, step):
    size = lax.axis_size(axes)
    return lax.ppermute(array, axes, [(i, (i + step) % size) for i in range(size)])


def pick(array, index):
    return lax.dynamic_index_in_dim(array, index, 0, keepdims=False)


def shifted(array, axes, destination):
    sizes = [lax.axis_size(name) for name in axes]
    pairs = []
    for index in np.ndindex(*sizes):
        goal = destination(*index)
        pairs.append((int(np.ravel_multi_index(index, sizes)), int(np.ravel_multi_index(goal, sizes))))
    return lax.ppermute(array, axes, pairs)


def after(array, other):
    return array + other[(0,) * other.ndim] * 0.0


def local(orbitals, kernel):
    xh, xl, y, core = [lax.axis_index(name) for name in ("xh", "xl", "y", "core")]
    place = jnp.stack([xl, y, core, xh]).astype(jnp.int32)
    table = jnp.asarray(make_table())

    def half(array, h):
        return lax.dynamic_slice_in_dim(array, h * (NY // 2), NY // 2, 2)

    with jax.named_scope("target_slabs"):
        def band(i, j):
            return pick(orbitals, 2 * (xl ^ i) + (core ^ j))

        came = moved(jnp.stack([band(0, 1), band(1, 1)]), "core", 1)
        across = moved(jnp.stack([band(1, 0), came[1]]), "xl", 1)
        part = jnp.stack([jnp.stack([band(0, 0), came[0]]), across])
        lower = moved(part, "y", 1)
        upper = moved(part, "y", -1)
        target_parts = [part, lower, moved(lower[0], "y", 1), moved(upper[1], "y", -1), upper]

    with jax.named_scope("source_slabs"):
        pieces = [pick(orbitals, y)]
        for r in range(1, 4):
            pieces.append(moved(pick(orbitals, (y + r) % 4), "y", r))
        own = after(jnp.stack(pieces), across)

    with jax.named_scope("source_fields"):
        own_other = moved(own, "xl", 1)
        far = moved(own, "z", 1)
        depth = lax.axis_size("z")
        near_other = shifted(own, ("z", "xh", "xl"), lambda k, h, l: ((k + h) % depth, 1 - h, 1 - l))
        near = moved(near_other, "xl", 1)
        far_other = moved(own_other, "z", 1)
        theirs = moved(half(orbitals, 1 - xh), "xh", 1)
        early, both = gather_early(place, orbitals, theirs, own, own_other, near_other, far, lower, upper)
        early = moved(early, "core", 1)

    with jax.named_scope("all_orbitals"):
        everything = lax.all_gather(both, "z", axis=0, tiled=True)

    own_field = [own, early[0], own_other, early[1]]
    total = pair_terms(place, target_parts, [own_field], kernel, table, None)
    late = moved(gather_late(near, far_other, total), "core", 1)
    rest = [[near, late[0], near_other, early[2]], [far, early[3], far_other, late[1]]]
    up, down, up_second, down_second, keep = pair_terms(place, target_parts, rest, kernel, table, total)

    with jax.named_scope("sum_partials"):
        low = moved(up, "y", 1)
        high = moved(down, "y", -1)
        zero = keep[0] + high[1] + moved(up_second + low[0], "y", 1)
        one = keep[1] + low[1] + moved(down_second + high[0], "y", -1)

    with jax.named_scope("to_slabs"):
        came = moved(jnp.stack([zero[1], one[1]]), "core", 1)
        kept = jnp.stack([zero[0], came[0]])
        sent = jnp.stack([one[0], came[1]])
        across = moved(sent, "xl", 1)
        straight = moved(half(kept, 1 - xh), "xh", 1)
        skew = shifted(half(sent, 1 - xh), ("xh", "xl"), lambda h, l: (1 - h, 1 - l))
        theirs = jnp.concatenate([straight, skew])
        relative = jnp.concatenate([kept, across])
        here = 2 * xl + core
        exchange_terms = jnp.stack([pick(relative, b ^ here) for b in range(4)])

    with jax.named_scope("margin"):
        shares = margin_shares(place, exchange_terms, theirs, everything)
        got = lax.all_to_all(shares, ("xh", "xl", "y", "core"), split_axis=0, concat_axis=0, tiled=True)
        margin = jnp.sum(got, axis=0).reshape(64, 4)
    return exchange_terms, margin


def solution(mesh):
    fine = Mesh(mesh.devices.reshape(8, 2, 2, 4, 2), ("z", "xh", "xl", "y", "core"))
    blk = ("z", "xh")
    slab = ("xl", "y", "core")
    return jax.shard_map(
        local,
        mesh=fine,
        in_specs=(P(blk, slab, None, None), P()),
        out_specs=(P(blk, slab, None, None), P(None, blk)),
        check_vma=False,
    )
```

profile of v0, /device:TPU:1, one launch (start us, length us, event | category | flops | bytes accessed | tf_op | source)
XLA Modules:
  0.0 190.7 jit_solution(625350859926062190)
XLA Ops:
  7.3 1.5 constant_dynamic-slice_fusion.5
  8.8 3.3 %collective-permute-start = (f32[2,3,48,240]{3,2,1,0:T(8,128)S(1)}, f32[2,3,48,240]{3,2,1,0:T(8,128)S(1)}, u32[]{:S(2)}, u32[]{:S(2)}) collective-permute-start(f32[2,3,48,240]{3,2,1,0:T(8,128)S(1)} %pad_maximum_fusion.4), channel_id=1, source_target_pairs={{0,1},{1,0},{2,3},{3,2},{4,5},{5,4},{6,7},{7,6},{8,9},{9,8},{10,11... | collective-permute-start | bytes 829448 | tf_op jit(solution)/shard_map/target_slabs/ppermute | solution.py:377
  13.5 2.4 %collective-permute-start.7 = (f32[3,48,240]{2,1,0:T(8,128)S(1)}, f32[3,48,240]{2,1,0:T(8,128)S(1)}, u32[]{:S(2)}, u32[]{:S(2)}) collective-permute-start(f32[3,48,240]{2,1,0:T(8,128)S(1)} %get-tuple-element.34), channel_id=1, source_target_pairs={{0,4},{2,6},{4,0},{6,2},{1,5},{3,7},{5,1},{7,3},{8,12},{10,14},{12... | collective-permute-start | bytes 414728 | tf_op jit(solution)/shard_map/source_slabs/ppermute | solution.py:377
  17.4 2.5 %collective-permute-start.13 = (f32[4,3,24,240]{3,2,1,0:T(8,128)S(1)}, f32[4,3,24,240]{3,2,1,0:T(8,128)S(1)}, u32[]{:S(2)}, u32[]{:S(2)}) collective-permute-start(f32[4,3,24,240]{3,2,1,0:T(8,128)S(1)} %constant_dynamic-slice_fusion.4), channel_id=1, source_target_pairs={{0,16},{16,0},{1,17},{17,1},{2,18},{18,2},{3,19},{19,3},{4,20},{20... | collective-permute-start | bytes 829448 | tf_op jit(solution)/shard_map/source_fields/ppermute | solution.py:377
  19.9 1.8 collective-permute-done.1
  23.2 1.7 collective-permute-start.11
  24.9 2.4 %collective-permute-start.9 = (f32[4,3,48,240]{3,2,1,0:T(8,128)S(1)}, f32[4,3,48,240]{3,2,1,0:T(8,128)S(1)}, u32[]{:S(2)}, u32[]{:S(2)}) collective-permute-start(f32[4,3,48,240]{3,2,1,0:T(8,128)S(1)} %maximum_add_fusion.own.refs_8_), channel_id=1, source_target_pairs={{0,24},{8,16},{16,40},{24,32},{32,56},{40,48},{48,72},{56,64},{64,... | collective-permute-start | bytes 1658888 | tf_op jit(solution)/shard_map/source_fields/ppermute | solution.py:390
  27.3 2.0 %collective-permute-start.2 = (f32[2,2,3,48,240]{4,3,2,1,0:T(8,128)S(1)}, f32[2,2,3,48,240]{4,3,2,1,0:T(8,128)S(1)}, u32[]{:S(2)}, u32[]{:S(2)}) collective-permute-start(f32[2,2,3,48,240]{4,3,2,1,0:T(8,128)S(1)} %pad_maximum_fusion.refs_3_), channel_id=1, source_target_pairs={{0,2},{2,4},{4,6},{6,0},{1,3},{3,5},{5,7},{7,1},{8,10},{10,12},{12... | collective-permute-start | bytes 1658888 | tf_op jit(solution)/shard_map/target_slabs/ppermute | solution.py:377
  29.3 1.9 collective-permute-start.4
  31.3 9.4 %collective-permute-done.11.own_other.refs_10_ = f32[4,3,48,240]{3,2,1,0:T(8,128)S(1)} collective-permute-done((f32[4,3,48,240]{3,2,1,0:T(8,128)S(1)}, f32[4,3,48,240]{3,2,1,0:T(8,128)S(1)}, u32[]{:S(2)}, u32[]{:S(2)}) %collective-permute-start.11) | collective-permute-done | bytes 552992 | tf_op jit(solution)/shard_map/source_fields/ppermute | solution.py:377
  40.7 14.5 %collective-permute-done.9.near_other.refs_10_ = f32[4,3,48,240]{3,2,1,0:T(8,128)S(1)} collective-permute-done((f32[4,3,48,240]{3,2,1,0:T(8,128)S(1)}, f32[4,3,48,240]{3,2,1,0:T(8,128)S(1)}, u32[]{:S(2)}, u32[]{:S(2)}) %collective-permute-start.9) | collective-permute-done | bytes 552992 | tf_op jit(solution)/shard_map/source_fields/ppermute | solution.py:390
  56.8 1.4 copy-done.12
  58.3 2.8 %collective-permute-start.15 = (f32[4,4,3,48,240]{4,3,2,1,0:T(8,128)}, f32[4,4,3,48,240]{4,3,2,1,0:T(8,128)S(1)}, u32[]{:S(2)}, u32[]{:S(2)}) collective-permute-start(f32[4,4,3,48,240]{4,3,2,1,0:T(8,128)} %copy-done.12), channel_id=1, source_target_pairs={{0,1},{1,0},{2,3},{3,2},{4,5},{5,4},{6,7},{7,6},{8,9},{9,8},{10,11... | collective-permute-start | bytes 6635528 | tf_op jit(solution)/shard_map/source_fields/ppermute | solution.py:377
  61.2 2.0 %collective-permute-start.3 = (f32[2,3,48,240]{3,2,1,0:T(8,128)S(1)}, f32[2,3,48,240]{3,2,1,0:T(8,128)S(1)}, u32[]{:S(2)}, u32[]{:S(2)}) collective-permute-start(f32[2,3,48,240]{3,2,1,0:T(8,128)S(1)} %slice_bitcast_fusion.9), channel_id=1, source_target_pairs={{0,2},{2,4},{4,6},{6,0},{1,3},{3,5},{5,7},{7,1},{8,10},{10,12},{12... | collective-permute-start | bytes 829448 | tf_op jit(solution)/shard_map/target_slabs/ppermute | solution.py:377
  63.2 1.7 collective-permute-start.5
  65.4 1.4 slice_bitcast_fusion.1
  66.9 5.0 %collective-permute-done.3.refs_5_ = f32[2,3,48,240]{3,2,1,0:T(8,128)S(1)} collective-permute-done((f32[2,3,48,240]{3,2,1,0:T(8,128)S(1)}, f32[2,3,48,240]{3,2,1,0:T(8,128)S(1)}, u32[]{:S(2)}, u32[]{:S(2)}) %collective-permute-start.3) | collective-permute-done | bytes 276512 | tf_op jit(solution)/shard_map/target_slabs/ppermute | solution.py:377
  72.7 12.2 %pair_terms.2.total.refs_16_ = f32[48,48,240]{2,1,0:T(8,128)} custom-call(s32[4]{0:T(128)} %copy-done.11, bf16[1248,768]{1,0:T(8,128)(2,1)} %constant.78.clone.refs_1_, f32[48,48,240]{2,1,0:T(8,128)} %refs_2_.3, f32[2,2,3,48,240]{4,3,2,1,0:T(8,128)} %copy-done.13, f32[2,2,3,48,240]{4,3,2,1,0:T(8,128)} %copy-done.2, f32[2,3,48,240]{3,2,1,0:T(8,128)} %copy-done.14, ...), custom_call_target="tpu_custom_call" | custom-call | flops 1000 | bytes 1000 | tf_op jit(solution)/shard_map/pair_terms/pallas_call | solution.py:254
  84.9 1.9 copy-done
  88.5 2.5 %collective-permute-done.16 = f32[2,4,3,48,240]{4,3,2,1,0:T(8,128)S(1)} collective-permute-done((f32[2,4,3,48,240]{4,3,2,1,0:T(8,128)S(1)}, f32[2,4,3,48,240]{4,3,2,1,0:T(8,128)S(1)}, u32[]{:S(2)}, u32[]{:S(2)}) %collective-permute-start.16) | collective-permute-done | bytes 1105952 | tf_op jit(solution)/shard_map/ppermute | solution.py:377
  92.2 21.1 %pair_terms.3 = (f32[2,2,3,48,240]{4,3,2,1,0:T(8,128)}, f32[2,2,3,48,240]{4,3,2,1,0:T(8,128)}, f32[2,3,48,240]{3,2,1,0:T(8,128)}, f32[2,3,48,240]{3,2,1,0:T(8,128)}, f32[2,2,3,48,240]{4,3,2,1,0:T(8,128)}) custom-call(s32[4]{0:T(128)} %copy-done.11, bf16[1248,768]{1,0:T(8,128)(2,1)} %constant.78.clone.refs_1_, f32[48,48,240]{2,1,0:T(8,128)} %refs_2_.3, ...), custom_call_target="tpu_custom_call" | custom-call | flops 1000 | bytes 1000 | tf_op jit(solution)/shard_map/pair_terms/pallas_call | solution.py:254
  113.2 2.8 %collective-permute-start.17 = (f32[2,2,3,48,240]{4,3,2,1,0:T(8,128)}, f32[2,2,3,48,240]{4,3,2,1,0:T(8,128)S(1)}, u32[]{:S(2)}, u32[]{:S(2)}) collective-permute-start(f32[2,2,3,48,240]{4,3,2,1,0:T(8,128)} %get-tuple-element.11), channel_id=1, source_target_pairs={{0,6},{2,0},{4,2},{6,4},{1,7},{3,1},{5,3},{7,5},{8,14},{10,8},{12,... | collective-permute-start | bytes 1658888 | tf_op jit(solution)/shard_map/sum_partials/ppermute | solution.py:377
  116.0 12.7 %collective-permute-done.17 = f32[2,2,3,48,240]{4,3,2,1,0:T(8,128)S(1)} collective-permute-done((f32[2,2,3,48,240]{4,3,2,1,0:T(8,128)}, f32[2,2,3,48,240]{4,3,2,1,0:T(8,128)S(1)}, u32[]{:S(2)}, u32[]{:S(2)}) %collective-permute-start.17) | collective-permute-done | bytes 552992 | tf_op jit(solution)/shard_map/sum_partials/ppermute | solution.py:377
  129.7 3.4 %collective-permute-start.20 = (f32[2,3,48,240]{3,2,1,0:T(8,128)S(1)}, f32[2,3,48,240]{3,2,1,0:T(8,128)S(1)}, u32[]{:S(2)}, u32[]{:S(2)}) collective-permute-start(f32[2,3,48,240]{3,2,1,0:T(8,128)S(1)} %fusion), channel_id=1, source_target_pairs={{0,6},{2,0},{4,2},{6,4},{1,7},{3,1},{5,3},{7,5},{8,14},{10,8},{12,... | collective-permute-start | bytes 829448 | tf_op jit(solution)/shard_map/sum_partials/ppermute | solution.py:377
  134.1 4.0 %collective-permute-done.20 = f32[2,3,48,240]{3,2,1,0:T(8,128)S(1)} collective-permute-done((f32[2,3,48,240]{3,2,1,0:T(8,128)S(1)}, f32[2,3,48,240]{3,2,1,0:T(8,128)S(1)}, u32[]{:S(2)}, u32[]{:S(2)}) %collective-permute-start.20) | collective-permute-done | bytes 276512 | tf_op jit(solution)/shard_map/sum_partials/ppermute | solution.py:377
  138.1 4.2 %collective-permute-done.19 = f32[2,3,48,240]{3,2,1,0:T(8,128)S(1)} collective-permute-done((f32[2,3,48,240]{3,2,1,0:T(8,128)S(1)}, f32[2,3,48,240]{3,2,1,0:T(8,128)S(1)}, u32[]{:S(2)}, u32[]{:S(2)}) %collective-permute-start.19) | collective-permute-done | bytes 276512 | tf_op jit(solution)/shard_map/sum_partials/ppermute | solution.py:377
  143.6 2.5 %collective-permute-start.21 = (f32[2,3,48,240]{3,2,1,0:T(8,128)S(1)}, f32[2,3,48,240]{3,2,1,0:T(8,128)S(1)}, u32[]{:S(2)}, u32[]{:S(2)}) collective-permute-start(f32[2,3,48,240]{3,2,1,0:T(8,128)S(1)} %pad_maximum_fusion.6), channel_id=1, source_target_pairs={{0,1},{1,0},{2,3},{3,2},{4,5},{5,4},{6,7},{7,6},{8,9},{9,8},{10,11... | collective-permute-start | bytes 829448 | tf_op jit(solution)/shard_map/to_slabs/ppermute | solution.py:377
  147.4 1.5 collective-permute-start.22
  149.0 2.5 %collective-permute-start.24 = (f32[2,3,24,240]{3,2,1,0:T(8,128)S(1)}, f32[2,3,24,240]{3,2,1,0:T(8,128)S(1)}, u32[]{:S(2)}, u32[]{:S(2)}) collective-permute-start(f32[2,3,24,240]{3,2,1,0:T(8,128)S(1)} %fusion.7), channel_id=1, source_target_pairs={{0,24},{8,16},{16,8},{24,0},{1,25},{9,17},{17,9},{25,1},{2,26},{10... | collective-permute-start | bytes 414728 | tf_op jit(solution)/shard_map/to_slabs/ppermute | solution.py:390
  151.4 6.6 %collective-permute-done.23 = f32[2,3,24,240]{3,2,1,0:T(8,128)S(1)} collective-permute-done((f32[2,3,24,240]{3,2,1,0:T(8,128)S(1)}, f32[2,3,24,240]{3,2,1,0:T(8,128)S(1)}, u32[]{:S(2)}, u32[]{:S(2)}) %collective-permute-start.23) | collective-permute-done | bytes 138272 | tf_op jit(solution)/shard_map/to_slabs/ppermute | solution.py:377
  160.3 7.2 %margin_shares.1 = f32[32,4,64]{2,1,0:T(4,128)} custom-call(s32[4]{0:T(128)} %copy-done.11, f32[4,3,48,240]{3,2,1,0:T(8,128)} %pad_maximum_fusion.2.terms, f32[4,3,24,240]{3,2,1,0:T(8,128)} %pad_maximum_fusion.7.theirs, f32[64,3,24,240]{3,2,1,0:T(8,128)} %all-gather.2.cloned.1.call-done.orbitals), custom_call_target="tpu_custom_call" | custom-call | flops 1000 | bytes 1000 | tf_op jit(solution)/shard_map/margin/margin_shares/pallas_call | solution.py:357
  168.5 13.2 %all_to_all.5 = f32[32,1,256]{2,1,0:T(1,128)S(1)} all-to-all(f32[32,1,256]{2,1,0:T(1,128)S(1)} %reshape.12), channel_id=1, replica_groups=mesh['z'=8,'xh'=2,'xl'=2,'y'=4,'core'=2] {'xh','xl','y','core'}, dimensions={0} | all-to-all | bytes 65536 | tf_op jit(solution)/shard_map/margin/all_to_all | solution.py:462
  (93 shorter events, 19.9 us)
Async XLA Ops:
  7.2 10.2 %copy-start.1 = (f32[4,3,48,240]{3,2,1,0:T(8,128)S(1)}, f32[4,3,48,240]{3,2,1,0:T(8,128)}, u32[]{:S(2)}) copy-start(f32[4,3,48,240]{3,2,1,0:T(8,128)} %orbitals.1) | copy-start | bytes 1658884
  7.2 153.2 %all-gather.2.cloned.1.call-start = ((), (), s32[]{:S(2)}) async-start(), calls=%async_computation.1 | async-start | bytes 5308416 | tf_op jit(solution)/shard_map/all_orbitals/all_gather | solution.py:434
  8.8 4.5 %collective-permute-start = (f32[2,3,48,240]{3,2,1,0:T(8,128)S(1)}, f32[2,3,48,240]{3,2,1,0:T(8,128)S(1)}, u32[]{:S(2)}, u32[]{:S(2)}) collective-permute-start(f32[2,3,48,240]{3,2,1,0:T(8,128)S(1)} %pad_maximum_fusion.4), channel_id=1, source_target_pairs={{0,1},{1,0},{2,3},{3,2},{4,5},{5,4},{6,7},{7,6},{8,9},{9,8},{10,11... | collective-permute-start | bytes 829448 | tf_op jit(solution)/shard_map/target_slabs/ppermute | solution.py:377
  13.4 8.3 %collective-permute-start.1 = (f32[2,3,48,240]{3,2,1,0:T(8,128)S(1)}, f32[2,3,48,240]{3,2,1,0:T(8,128)S(1)}, u32[]{:S(2)}, u32[]{:S(2)}) collective-permute-start(f32[2,3,48,240]{3,2,1,0:T(8,128)S(1)} %pad_maximum_fusion.5), channel_id=1, source_target_pairs={{0,8},{8,0},{1,9},{9,1},{2,10},{10,2},{3,11},{11,3},{4,12},{12,4},... | collective-permute-start | bytes 829448 | tf_op jit(solution)/shard_map/target_slabs/ppermute | solution.py:377
  13.5 9.4 %collective-permute-start.7 = (f32[3,48,240]{2,1,0:T(8,128)S(1)}, f32[3,48,240]{2,1,0:T(8,128)S(1)}, u32[]{:S(2)}, u32[]{:S(2)}) collective-permute-start(f32[3,48,240]{2,1,0:T(8,128)S(1)} %get-tuple-element.34), channel_id=1, source_target_pairs={{0,4},{2,6},{4,0},{6,2},{1,5},{3,7},{5,1},{7,3},{8,12},{10,14},{12... | collective-permute-start | bytes 414728 | tf_op jit(solution)/shard_map/source_slabs/ppermute | solution.py:377
  15.9 7.0 %collective-permute-start.8 = (f32[3,48,240]{2,1,0:T(8,128)S(1)}, f32[3,48,240]{2,1,0:T(8,128)S(1)}, u32[]{:S(2)}, u32[]{:S(2)}) collective-permute-start(f32[3,48,240]{2,1,0:T(8,128)S(1)} %get-tuple-element.33), channel_id=1, source_target_pairs={{0,6},{2,0},{4,2},{6,4},{1,7},{3,1},{5,3},{7,5},{8,14},{10,8},{12,... | collective-permute-start | bytes 414728 | tf_op jit(solution)/shard_map/source_slabs/ppermute | solution.py:377
  16.6 6.5 %collective-permute-start.6 = (f32[3,48,240]{2,1,0:T(8,128)S(1)}, f32[3,48,240]{2,1,0:T(8,128)S(1)}, u32[]{:S(2)}, u32[]{:S(2)}) collective-permute-start(f32[3,48,240]{2,1,0:T(8,128)S(1)} %get-tuple-element.35), channel_id=1, source_target_pairs={{0,2},{2,4},{4,6},{6,0},{1,3},{3,5},{5,7},{7,1},{8,10},{10,12},{12... | collective-permute-start | bytes 414728 | tf_op jit(solution)/shard_map/source_slabs/ppermute | solution.py:377
  17.4 12.0 %collective-permute-start.13 = (f32[4,3,24,240]{3,2,1,0:T(8,128)S(1)}, f32[4,3,24,240]{3,2,1,0:T(8,128)S(1)}, u32[]{:S(2)}, u32[]{:S(2)}) collective-permute-start(f32[4,3,24,240]{3,2,1,0:T(8,128)S(1)} %constant_dynamic-slice_fusion.4), channel_id=1, source_target_pairs={{0,16},{16,0},{1,17},{17,1},{2,18},{18,2},{3,19},{19,3},{4,20},{20... | collective-permute-start | bytes 829448 | tf_op jit(solution)/shard_map/source_fields/ppermute | solution.py:377
  23.2 32.8 %copy-start.4 = (f32[4,3,48,240]{3,2,1,0:T(8,128)}, f32[4,3,48,240]{3,2,1,0:T(8,128)S(1)}, u32[]{:S(2)}) copy-start(f32[4,3,48,240]{3,2,1,0:T(8,128)S(1)} %maximum_add_fusion.own.refs_8_) | copy-start | bytes 1658884
  23.2 17.4 %collective-permute-start.11 = (f32[4,3,48,240]{3,2,1,0:T(8,128)S(1)}, f32[4,3,48,240]{3,2,1,0:T(8,128)S(1)}, u32[]{:S(2)}, u32[]{:S(2)}) collective-permute-start(f32[4,3,48,240]{3,2,1,0:T(8,128)S(1)} %maximum_add_fusion.own.refs_8_), channel_id=1, source_target_pairs={{0,8},{8,0},{1,9},{9,1},{2,10},{10,2},{3,11},{11,3},{4,12},{12,4},... | collective-permute-start | bytes 1658888 | tf_op jit(solution)/shard_map/source_fields/ppermute | solution.py:377
  24.9 15.8 %collective-permute-start.14 = (f32[4,3,48,240]{3,2,1,0:T(8,128)S(1)}, f32[4,3,48,240]{3,2,1,0:T(8,128)S(1)}, u32[]{:S(2)}, u32[]{:S(2)}) collective-permute-start(f32[4,3,48,240]{3,2,1,0:T(8,128)S(1)} %maximum_add_fusion.own.refs_8_), channel_id=1, source_target_pairs={{0,32},{32,64},{64,96},{96,128},{128,160},{160,192},{192,224},{224... | collective-permute-start | bytes 1658888 | tf_op jit(solution)/shard_map/source_fields/ppermute | solution.py:377
  24.9 30.3 %collective-permute-start.9 = (f32[4,3,48,240]{3,2,1,0:T(8,128)S(1)}, f32[4,3,48,240]{3,2,1,0:T(8,128)S(1)}, u32[]{:S(2)}, u32[]{:S(2)}) collective-permute-start(f32[4,3,48,240]{3,2,1,0:T(8,128)S(1)} %maximum_add_fusion.own.refs_8_), channel_id=1, source_target_pairs={{0,24},{8,16},{16,40},{24,32},{32,56},{40,48},{48,72},{56,64},{64,... | collective-permute-start | bytes 1658888 | tf_op jit(solution)/shard_map/source_fields/ppermute | solution.py:390
  27.3 27.9 %copy-start.13 = (f32[2,2,3,48,240]{4,3,2,1,0:T(8,128)}, f32[2,2,3,48,240]{4,3,2,1,0:T(8,128)S(1)}, u32[]{:S(2)}) copy-start(f32[2,2,3,48,240]{4,3,2,1,0:T(8,128)S(1)} %pad_maximum_fusion.refs_3_) | copy-start | bytes 1658884
  27.3 27.9 %collective-permute-start.2 = (f32[2,2,3,48,240]{4,3,2,1,0:T(8,128)S(1)}, f32[2,2,3,48,240]{4,3,2,1,0:T(8,128)S(1)}, u32[]{:S(2)}, u32[]{:S(2)}) collective-permute-start(f32[2,2,3,48,240]{4,3,2,1,0:T(8,128)S(1)} %pad_maximum_fusion.refs_3_), channel_id=1, source_target_pairs={{0,2},{2,4},{4,6},{6,0},{1,3},{3,5},{5,7},{7,1},{8,10},{10,12},{12... | collective-permute-start | bytes 1658888 | tf_op jit(solution)/shard_map/target_slabs/ppermute | solution.py:377
  29.3 25.9 %collective-permute-start.4 = (f32[2,2,3,48,240]{4,3,2,1,0:T(8,128)S(1)}, f32[2,2,3,48,240]{4,3,2,1,0:T(8,128)S(1)}, u32[]{:S(2)}, u32[]{:S(2)}) collective-permute-start(f32[2,2,3,48,240]{4,3,2,1,0:T(8,128)S(1)} %pad_maximum_fusion.refs_3_), channel_id=1, source_target_pairs={{0,6},{2,0},{4,2},{6,4},{1,7},{3,1},{5,3},{7,5},{8,14},{10,8},{12,... | collective-permute-start | bytes 1658888 | tf_op jit(solution)/shard_map/target_slabs/ppermute | solution.py:377
  31.3 27.0 %copy-start.11 = (s32[4]{0:T(128)}, s32[4]{0:T(128)S(1)}, u32[]{:S(2)}) copy-start(s32[4]{0:T(128)S(1)} %pad_add_fusion.place.refs_0_) | copy-start | bytes 52
  40.7 20.4 %copy-start.5 = (f32[4,3,48,240]{3,2,1,0:T(8,128)}, f32[4,3,48,240]{3,2,1,0:T(8,128)S(1)}, u32[]{:S(2)}) copy-start(f32[4,3,48,240]{3,2,1,0:T(8,128)S(1)} %collective-permute-done.11.own_other.refs_10_) | copy-start | bytes 1658884
  40.7 17.6 %copy-start.6 = (f32[4,3,48,240]{3,2,1,0:T(8,128)}, f32[4,3,48,240]{3,2,1,0:T(8,128)S(1)}, u32[]{:S(2)}) copy-start(f32[4,3,48,240]{3,2,1,0:T(8,128)S(1)} %collective-permute-done.14.far.refs_12_) | copy-start | bytes 1658884
  58.3 7.1 %collective-permute-start.15 = (f32[4,4,3,48,240]{4,3,2,1,0:T(8,128)}, f32[4,4,3,48,240]{4,3,2,1,0:T(8,128)S(1)}, u32[]{:S(2)}, u32[]{:S(2)}) collective-permute-start(f32[4,4,3,48,240]{4,3,2,1,0:T(8,128)} %copy-done.12), channel_id=1, source_target_pairs={{0,1},{1,0},{2,3},{3,2},{4,5},{5,4},{6,7},{7,6},{8,9},{9,8},{10,11... | collective-permute-start | bytes 6635528 | tf_op jit(solution)/shard_map/source_fields/ppermute | solution.py:377
  61.1 23.8 %collective-permute-start.10 = (f32[4,3,48,240]{3,2,1,0:T(8,128)S(1)}, f32[4,3,48,240]{3,2,1,0:T(8,128)S(1)}, u32[]{:S(2)}, u32[]{:S(2)}) collective-permute-start(f32[4,3,48,240]{3,2,1,0:T(8,128)S(1)} %collective-permute-done.9.near_other.refs_10_), channel_id=1, source_target_pairs={{0,8},{8,0},{1,9},{9,1},{2,10},{10,2},{3,11},{11,3},{4,12},{12,4},... | collective-permute-start | bytes 1658888 | tf_op jit(solution)/shard_map/source_fields/ppermute | solution.py:377
  61.1 23.8 %collective-permute-start.12 = (f32[4,3,48,240]{3,2,1,0:T(8,128)S(1)}, f32[4,3,48,240]{3,2,1,0:T(8,128)S(1)}, u32[]{:S(2)}, u32[]{:S(2)}) collective-permute-start(f32[4,3,48,240]{3,2,1,0:T(8,128)S(1)} %collective-permute-done.11.own_other.refs_10_), channel_id=1, source_target_pairs={{0,32},{32,64},{64,96},{96,128},{128,160},{160,192},{192,224},{224... | collective-permute-start | bytes 1658888 | tf_op jit(solution)/shard_map/source_fields/ppermute | solution.py:377
  61.2 10.7 %collective-permute-start.3 = (f32[2,3,48,240]{3,2,1,0:T(8,128)S(1)}, f32[2,3,48,240]{3,2,1,0:T(8,128)S(1)}, u32[]{:S(2)}, u32[]{:S(2)}) collective-permute-start(f32[2,3,48,240]{3,2,1,0:T(8,128)S(1)} %slice_bitcast_fusion.9), channel_id=1, source_target_pairs={{0,2},{2,4},{4,6},{6,0},{1,3},{3,5},{5,7},{7,1},{8,10},{10,12},{12... | collective-permute-start | bytes 829448 | tf_op jit(solution)/shard_map/target_slabs/ppermute | solution.py:377
  63.2 8.6 %collective-permute-start.5 = (f32[2,3,48,240]{3,2,1,0:T(8,128)S(1)}, f32[2,3,48,240]{3,2,1,0:T(8,128)S(1)}, u32[]{:S(2)}, u32[]{:S(2)}) collective-permute-start(f32[2,3,48,240]{3,2,1,0:T(8,128)S(1)} %slice_bitcast_fusion.8), channel_id=1, source_target_pairs={{0,6},{2,0},{4,2},{6,4},{1,7},{3,1},{5,3},{7,5},{8,14},{10,8},{12,... | collective-permute-start | bytes 829448 | tf_op jit(solution)/shard_map/target_slabs/ppermute | solution.py:377
  87.6 3.4 %collective-permute-start.16 = (f32[2,4,3,48,240]{4,3,2,1,0:T(8,128)S(1)}, f32[2,4,3,48,240]{4,3,2,1,0:T(8,128)S(1)}, u32[]{:S(2)}, u32[]{:S(2)}) collective-permute-start(f32[2,4,3,48,240]{4,3,2,1,0:T(8,128)S(1)} %gather_late.1), channel_id=1, source_target_pairs={{0,1},{1,0},{2,3},{3,2},{4,5},{5,4},{6,7},{7,6},{8,9},{9,8},{10,11... | collective-permute-start | bytes 3317768 | tf_op jit(solution)/shard_map/ppermute | solution.py:377
  113.2 15.4 %collective-permute-start.17 = (f32[2,2,3,48,240]{4,3,2,1,0:T(8,128)}, f32[2,2,3,48,240]{4,3,2,1,0:T(8,128)S(1)}, u32[]{:S(2)}, u32[]{:S(2)}) collective-permute-start(f32[2,2,3,48,240]{4,3,2,1,0:T(8,128)} %get-tuple-element.11), channel_id=1, source_target_pairs={{0,6},{2,0},{4,2},{6,4},{1,7},{3,1},{5,3},{7,5},{8,14},{10,8},{12,... | collective-permute-start | bytes 1658888 | tf_op jit(solution)/shard_map/sum_partials/ppermute | solution.py:377
  116.0 17.0 %collective-permute-start.18 = (f32[2,2,3,48,240]{4,3,2,1,0:T(8,128)}, f32[2,2,3,48,240]{4,3,2,1,0:T(8,128)S(1)}, u32[]{:S(2)}, u32[]{:S(2)}) collective-permute-start(f32[2,2,3,48,240]{4,3,2,1,0:T(8,128)} %get-tuple-element.13), channel_id=1, source_target_pairs={{0,2},{2,4},{4,6},{6,0},{1,3},{3,5},{5,7},{7,1},{8,10},{10,12},{12... | collective-permute-start | bytes 1658888 | tf_op jit(solution)/shard_map/sum_partials/ppermute | solution.py:377
  129.7 8.5 %collective-permute-start.20 = (f32[2,3,48,240]{3,2,1,0:T(8,128)S(1)}, f32[2,3,48,240]{3,2,1,0:T(8,128)S(1)}, u32[]{:S(2)}, u32[]{:S(2)}) collective-permute-start(f32[2,3,48,240]{3,2,1,0:T(8,128)S(1)} %fusion), channel_id=1, source_target_pairs={{0,6},{2,0},{4,2},{6,4},{1,7},{3,1},{5,3},{7,5},{8,14},{10,8},{12,... | collective-permute-start | bytes 829448 | tf_op jit(solution)/shard_map/sum_partials/ppermute | solution.py:377
  134.0 8.3 %collective-permute-start.19 = (f32[2,3,48,240]{3,2,1,0:T(8,128)S(1)}, f32[2,3,48,240]{3,2,1,0:T(8,128)S(1)}, u32[]{:S(2)}, u32[]{:S(2)}) collective-permute-start(f32[2,3,48,240]{3,2,1,0:T(8,128)S(1)} %fusion.3), channel_id=1, source_target_pairs={{0,2},{2,4},{4,6},{6,0},{1,3},{3,5},{5,7},{7,1},{8,10},{10,12},{12... | collective-permute-start | bytes 829448 | tf_op jit(solution)/shard_map/sum_partials/ppermute | solution.py:377
  143.6 3.7 %collective-permute-start.21 = (f32[2,3,48,240]{3,2,1,0:T(8,128)S(1)}, f32[2,3,48,240]{3,2,1,0:T(8,128)S(1)}, u32[]{:S(2)}, u32[]{:S(2)}) collective-permute-start(f32[2,3,48,240]{3,2,1,0:T(8,128)S(1)} %pad_maximum_fusion.6), channel_id=1, source_target_pairs={{0,1},{1,0},{2,3},{3,2},{4,5},{5,4},{6,7},{7,6},{8,9},{9,8},{10,11... | collective-permute-start | bytes 829448 | tf_op jit(solution)/shard_map/to_slabs/ppermute | solution.py:377
  147.4 12.0 %collective-permute-start.22 = (f32[2,3,48,240]{3,2,1,0:T(8,128)S(1)}, f32[2,3,48,240]{3,2,1,0:T(8,128)S(1)}, u32[]{:S(2)}, u32[]{:S(2)}) collective-permute-start(f32[2,3,48,240]{3,2,1,0:T(8,128)S(1)} %pad_maximum_fusion.3), channel_id=1, source_target_pairs={{0,8},{8,0},{1,9},{9,1},{2,10},{10,2},{3,11},{11,3},{4,12},{12,4},... | collective-permute-start | bytes 829448 | tf_op jit(solution)/shard_map/to_slabs/ppermute | solution.py:377
  148.9 9.1 %collective-permute-start.23 = (f32[2,3,24,240]{3,2,1,0:T(8,128)S(1)}, f32[2,3,24,240]{3,2,1,0:T(8,128)S(1)}, u32[]{:S(2)}, u32[]{:S(2)}) collective-permute-start(f32[2,3,24,240]{3,2,1,0:T(8,128)S(1)} %fusion.6), channel_id=1, source_target_pairs={{0,16},{16,0},{1,17},{17,1},{2,18},{18,2},{3,19},{19,3},{4,20},{20... | collective-permute-start | bytes 414728 | tf_op jit(solution)/shard_map/to_slabs/ppermute | solution.py:377
  149.0 9.6 %collective-permute-start.24 = (f32[2,3,24,240]{3,2,1,0:T(8,128)S(1)}, f32[2,3,24,240]{3,2,1,0:T(8,128)S(1)}, u32[]{:S(2)}, u32[]{:S(2)}) collective-permute-start(f32[2,3,24,240]{3,2,1,0:T(8,128)S(1)} %fusion.7), channel_id=1, source_target_pairs={{0,24},{8,16},{16,8},{24,0},{1,25},{9,17},{17,9},{25,1},{2,26},{10... | collective-permute-start | bytes 414728 | tf_op jit(solution)/shard_map/to_slabs/ppermute | solution.py:390
  (10 other events, 28.3 us)
Sparse Core Ops, SparseCore 0:
  58.4 64.0 all-gather.1
where the time goes:
time: 191 us
  waiting for transfers between devices  64.4 us (34%)
  Pallas kernels  41.3 us (22%)
  starting transfers between devices  38 us (20%)
  between operations  15.1 us (8%)
  blocking collectives  13.2 us (7%)
  local copies, waits for them, and re-layouts  12.8 us (7%)
  other arithmetic  5.9 us (3%)
    ppermute x23, waiting for transfers between devices, moved(): lax.ppermute(array, axes, [(i, (i + step) % size) for i in range(size)])  49.3 us
    pallas_call x2, Pallas kernels, pair_terms(): pl.pallas_call(functools.partial(pair_kernel, count, last), out_shape=out...  33.2 us
    ppermute x23, starting transfers between devices, moved(): lax.ppermute(array, axes, [(i, (i + step) % size) for i in range(size)])  33.1 us
    ppermute x2, waiting for transfers between devices, shifted(): return lax.ppermute(array, axes, pairs)  15.1 us
    all_to_all x1, blocking collectives, local(): lax.all_to_all(shares, ('xh', 'xl', 'y', 'core'), split_axis=0, concat_ax...  13.2 us
    unnamed x35, local copies, waits for them, and re-layouts  7.45 us
    pallas_call x1, Pallas kernels, margin_shares(): pl.pallas_call(margin_kernel, grid=(4,), out_shape=jax.ShapeDtypeStruct((...  7.25 us
    ppermute x2, starting transfers between devices, shifted(): return lax.ppermute(array, axes, pairs)  4.83 us
  transfers between devices with their start and end apart: 26, of which 14 were waited for; matrix products, arithmetic and copies ran while one was open for 4% of the time, Pallas kernels for 17%

commit v1 on v0

v1 whole, which is shorter than its diff:
```python
import functools
import math

import jax
import jax.numpy as jnp
import ml_dtypes
import numpy as np
from jax import lax
from jax.experimental import pallas as pl
from jax.experimental.pallas import tpu as pltpu
from jax.sharding import Mesh, PartitionSpec as P

NX = 48
NY = 48
NZ = 240
LANES = 256
EVEN = 26
ODD = 24
GRID = NX * NY * NZ

bf16 = jnp.bfloat16
f32 = jnp.float32
highest = lax.Precision.HIGHEST


def halves(table):
    high = table.astype(ml_dtypes.bfloat16)
    low = (table - high.astype(np.float64)).astype(ml_dtypes.bfloat16)
    return high, low


def cas(length):
    position = np.arange(length)
    angles = (position[:, None] * position[None, :] % length) * (2.0 * math.pi / length)
    return np.cos(angles) + np.sin(angles)


def left_table(table):
    high, low = halves(table)
    return np.concatenate([high, low, high], axis=1)


WIDTH = 3 * LANES
ROWS = (LANES, 192, 8 * EVEN, 8 * ODD, 8 * EVEN, 8 * ODD)
FIRST = tuple(sum(ROWS[:k]) for k in range(len(ROWS) + 1))


def make_table():
    table_z = np.zeros((LANES, LANES))
    table_z[:NZ, :NZ] = cas(NZ)
    high, low = halves(table_z)
    along_z = np.concatenate([high, high, low], axis=1)
    along_y = left_table(np.kron(np.eye(4), cas(NY)))
    place = np.arange(NX // 2 + 1)
    angles = (place[:, None] * place[None, :] % NX) * (2.0 * math.pi / NX)
    even = np.zeros((EVEN, EVEN))
    even[:25, :25] = np.cos(angles)
    odd = np.zeros((ODD, ODD))
    odd[:24, :24] = np.sin(angles)[:24, :24]
    weight = np.full(EVEN, 2.0)
    weight[0] = weight[24] = 1.0
    eye = np.eye(8)
    even_there = left_table(np.kron(even, eye))
    odd_there = left_table(np.kron(odd, eye))
    even_back = left_table(np.kron(even * weight[None, :] * (-1.0 / GRID), eye))
    odd_back = left_table(np.kron(odd * (-2.0 / GRID), eye))
    table = np.zeros((FIRST[-1], WIDTH), ml_dtypes.bfloat16)
    parts = (along_z, along_y, even_there, odd_there, even_back, odd_back)
    for first, part in zip(FIRST, parts):
        table[first : first + part.shape[0], : part.shape[1]] = part
    return table


def split(value):
    high = value.astype(bf16)
    low = (value - high.astype(f32)).astype(bf16)
    return high, low


def from_right(rows, table):
    high, low = split(rows)
    result = jnp.dot(high, table[0:LANES, 0:LANES], preferred_element_type=f32)
    result += jnp.dot(low, table[0:LANES, LANES : 2 * LANES], preferred_element_type=f32)
    return result + jnp.dot(high, table[0:LANES, 2 * LANES :], preferred_element_type=f32)


def from_left(table, k, rows):
    high, low = split(rows)
    stacked = jnp.concatenate([high, high, low], axis=0)
    return jnp.dot(
        table[FIRST[k] : FIRST[k + 1], : stacked.shape[0]], stacked, preferred_element_type=f32
    )


def widen(value):
    return jnp.pad(value, [(0, 0)] * (value.ndim - 1) + [(0, LANES - NZ)])


def pair_kernel(*refs):
    place, table_hbm, filt_hbm = refs[:3]
    target_parts = refs[3:8]
    field_parts = [refs[8 + 4 * s : 12 + 4 * s] for s in range(3)]
    up_first, down_first, up_second, down_second, keep = refs[20:25]
    targets, sources, source, product, planes, total, table, filt, sems = refs[25:]
    xl, y, core = place[0], place[1], place[2]

    table_copy = pltpu.make_async_copy(table_hbm, table, sems.at[3, 0])
    filt_copy = pltpu.make_async_copy(filt_hbm.at[pl.ds(0, EVEN)], filt, sems.at[3, 1])
    homes = (targets.at[0], targets.at[1], targets.at[2, 0], targets.at[2, 1], targets.at[3])
    target_copies = [
        pltpu.make_async_copy(ref, goal, sems.at[4, n]) for n, (ref, goal) in enumerate(zip(target_parts, homes))
    ]
    target_groups = (target_copies[0:1], target_copies[1:2], target_copies[2:4], target_copies[4:5])
    source_copies = [
        [pltpu.make_async_copy(ref.at[r], sources.at[s, r, q], sems.at[s, r]) for q, ref in enumerate(parts)]
        for s, parts in enumerate(field_parts)
        for r in range(4)
    ]
    for r in range(4):
        for copy in target_groups[r]:
            copy.start()
        for copy in source_copies[r]:
            copy.start()
    table_copy.start()
    filt_copy.start()
    for group in source_copies[4:]:
        for copy in group:
            copy.start()

    def base(i, r, j):
        return (xl ^ i) * 24 + ((y + r) % 4) * 6 + (core ^ j) * 3

    pieces = [(r, i, j) for r in range(4) for i in range(2) for j in range(2)]
    planes[25] = jnp.zeros((NY, LANES), f32)
    planes[EVEN] = jnp.zeros((NY, LANES), f32)
    total[...] = jnp.zeros_like(total)

    def members(k):
        if k < 11:
            a = 2 * k + 1
            return (a, a + 1, EVEN + a, EVEN + a + 1)
        return (0, 24, 23, EVEN + 23)

    def products(s):
        for r in range(4):

            @pl.when(s == 0)
            def _():
                for copy in target_groups[r]:
                    copy.wait()

            for q in range(4):
                pltpu.make_async_copy(sources.at[s, r, q], sources.at[s, r, q], sems.at[s, r]).wait()
            for i in range(2):
                for j in range(2):
                    start = base(i, 4 - r, j)
                    values = sources[s, r, 2 * i + j]
                    source[pl.ds(start, 3)] = values
                    product[pl.ds(start, 3)] = values * targets[r, i, j]

    def visit(s):
        for k in range(12):
            if k < 11:
                a = 2 * k + 1
                fa, ga, fb, gb = (product[x] for x in (a, NX - a, a + 1, NX - a - 1))
                rows = [fa + ga, fb + gb, fa - ga, fb - gb]
            else:
                fa, ga = product[23], product[25]
                rows = [product[0], product[24], fa + ga, fa - ga]
            rows = widen(jnp.concatenate(rows, axis=0))
            rows = from_right(rows, table)
            rows = from_left(table, 1, rows).reshape(4, NY, LANES)
            for m, plane in enumerate(members(k)):
                planes[plane] = rows[m]

        for t in range(6):
            band = pl.ds(8 * t, 8)
            screen = widen(filt[0:EVEN, band, :])
            for there, back, lo, size in ((2, 4, 0, EVEN), (3, 5, EVEN, ODD)):
                rows = planes[lo : lo + size, band, :].reshape(size * 8, LANES)
                rows = from_left(table, there, rows)
                rows = rows * screen[:size].reshape(size * 8, LANES)
                rows = from_left(table, back, rows)
                planes[lo : lo + size, band, :] = rows.reshape(size, 8, LANES)

        def add(x, value):
            value = value[:, :NZ] * source[x]
            total[x] += value

        for k in range(12):
            rows = jnp.concatenate([planes[plane] for plane in members(k)], axis=0)
            rows = from_left(table, 1, rows)
            rows = from_right(rows, table).reshape(4, NY, LANES)
            if k < 11:
                a = 2 * k + 1
                for m in range(2):
                    add(a + m, rows[m] + rows[m + 2])
                    add(NX - a - m, rows[m] - rows[m + 2])
            else:
                add(0, rows[0])
                add(24, rows[1])
                add(23, rows[2] + rows[3])
                add(25, rows[2] - rows[3])

    @pl.loop(0, 3)
    def _(s):
        products(s)

        @pl.when(s == 0)
        def _():
            table_copy.wait()
            filt_copy.wait()

        visit(s)

    homes = {
        (0, 0): keep.at[0], (0, 1): keep.at[1],
        (1, 0): up_second, (1, 1): up_first.at[1],
        (2, 0): up_first.at[0], (2, 1): down_first.at[0],
        (3, 0): down_first.at[1], (3, 1): down_second,
    }
    copies = [
        pltpu.make_async_copy(total.at[pl.ds(base(i, r, j), 3)], homes[r, i].at[j], sems.at[3, 2])
        for r, i, j in pieces
    ]
    for copy in copies:
        copy.start()
    for copy in copies:
        copy.wait()


def pair_terms(place, target_parts, fields, kernel, table):
    operands = [place, table, kernel, *target_parts, *[part for field in fields for part in field]]
    whole = jax.ShapeDtypeStruct((2, 2, 3, NY, NZ), f32)
    piece = jax.ShapeDtypeStruct((2, 3, NY, NZ), f32)
    hbm = pl.BlockSpec(memory_space=pl.ANY)
    return pl.pallas_call(
        pair_kernel,
        out_shape=[whole, whole, piece, piece, whole],
        in_specs=[pl.BlockSpec(memory_space=pltpu.SMEM)] + [hbm] * (len(operands) - 1),
        out_specs=[hbm] * 5,
        scratch_shapes=[
            pltpu.VMEM((4, 2, 2, 3, NY, NZ), f32),
            pltpu.VMEM((3, 4, 4, 3, NY, NZ), f32),
            pltpu.VMEM((NX, NY, NZ), f32),
            pltpu.VMEM((NX, NY, NZ), f32),
            pltpu.VMEM((EVEN + ODD, NY, LANES), f32),
            pltpu.VMEM((NX, NY, NZ), f32),
            pltpu.VMEM((FIRST[-1], WIDTH), bf16),
            pltpu.VMEM((EVEN, NY, NZ), f32),
            pltpu.SemaphoreType.DMA((5, 5)),
        ],
        compiler_params=pltpu.CompilerParams(vmem_limit_bytes=60 * 2**20),
        cost_estimate=pl.CostEstimate(flops=1000, bytes_accessed=1000, transcendentals=0),
        name="pair_terms",
    )(*operands)


def halves_kernel(place, orbitals, theirs, *refs):
    both, sems = refs[-2:]
    xh = place[3]
    mine = orbitals.at[:, :, pl.ds(pl.multiple_of(24 * xh, 8), 24), :]
    copies = [
        pltpu.make_async_copy(mine, both.at[pl.ds(4 * xh, 4)], sems.at[0]),
        pltpu.make_async_copy(theirs, both.at[pl.ds(4 * (1 - xh), 4)], sems.at[1]),
    ]
    for copy in copies:
        copy.start()
    for copy in copies:
        copy.wait()


def both_halves(place, orbitals, theirs, *events):
    vmem = pl.BlockSpec(memory_space=pltpu.VMEM)
    hbm = pl.BlockSpec(memory_space=pl.ANY)
    return pl.pallas_call(
        halves_kernel,
        out_shape=jax.ShapeDtypeStruct((8, 3, NY // 2, NZ), f32),
        in_specs=[pl.BlockSpec(memory_space=pltpu.SMEM), vmem, vmem] + [hbm] * len(events),
        out_specs=hbm,
        scratch_shapes=[pltpu.SemaphoreType.DMA((2,))],
        compiler_params=pltpu.CompilerParams(vmem_limit_bytes=60 * 2**20),
        cost_estimate=pl.CostEstimate(flops=1000, bytes_accessed=1000, transcendentals=0),
        name="both_halves",
    )(place, orbitals, theirs, *events)


def margin_kernel(place, kept, across, straight, skew, orbitals, shares, exchange, sums, lines, sems):
    here = 2 * place[0] + place[2]
    xh = place[3]
    step = pl.program_id(0)
    copies = [
        pltpu.make_async_copy(pair.at[b], exchange.at[(2 * a + b) ^ here], sems.at[2 * a + b])
        for a, pair in enumerate((kept, across))
        for b in range(2)
    ]

    @pl.when(step == 0)
    def _():
        for copy in copies:
            copy.start()

    @pl.loop(0, 16)
    def _(p):
        totals = [[None] * 8 for _ in range(2)]
        for x in range(3):
            for t in range(3):
                rows = pl.ds(8 * t, 8)
                mine = pl.ds(pl.multiple_of(xh * 24 + 8 * t, 8), 8)
                values = [orbitals[2 * p + m, x, rows, :] for m in range(2)]
                terms = [kept[0, x, mine, :], kept[1, x, mine, :], across[0, x, mine, :], across[1, x, mine, :]]
                terms += [straight[0, x, rows, :], straight[1, x, rows, :], skew[0, x, rows, :], skew[1, x, rows, :]]
                for k in range(8):
                    for m in range(2):
                        value = terms[k] * values[m]
                        totals[m][k] = value if totals[m][k] is None else totals[m][k] + value
        for m in range(2):
            for k in range(8):
                sums[k // 4, 2 * p + m, (k % 4) ^ here] = totals[m][k]

    rows = sums[...].reshape(2048, NZ) * (1.0 / GRID)
    high, low = split(rows)
    ones = jnp.ones((NZ, 128), bf16)
    rows = jnp.dot(high, ones, preferred_element_type=f32)
    rows += jnp.dot(low, ones, preferred_element_type=f32)
    rows = jnp.sum(rows.reshape(256, 8, 128), axis=1)
    place_of = lax.broadcasted_iota(jnp.int32, (128, 128), 0)
    lane_of = lax.broadcasted_iota(jnp.int32, (128, 128), 1)
    for g in range(2):
        line = jnp.where(place_of == lane_of, rows[128 * g : 128 * g + 128], 0.0)
        lines[g, pl.ds(step, 1)] = jnp.sum(line, axis=0, keepdims=True)

    @pl.when(step == 1)
    def _():
        for g in range(2):
            for n in range(2):
                row = jnp.broadcast_to(lines[g, n : n + 1], (16, 128))
                shares[pl.ds((xh ^ g) * 16, 16), 0, 128 * n : 128 * n + 128] = row
        for copy in copies:
            copy.wait()


def margin_shares(place, kept, across, straight, skew, orbitals):
    vmem = pl.BlockSpec(memory_space=pltpu.VMEM)
    return pl.pallas_call(
        margin_kernel,
        grid=(2,),
        out_shape=[
            jax.ShapeDtypeStruct((32, 1, 256), f32),
            jax.ShapeDtypeStruct((4, 3, NY, NZ), f32),
        ],
        in_specs=[pl.BlockSpec(memory_space=pltpu.SMEM)]
        + [vmem] * 4
        + [pl.BlockSpec((32, 3, NY // 2, NZ), lambda z: (z, 0, 0, 0))],
        out_specs=[
            pl.BlockSpec((32, 1, 256), lambda z: (0, 0, 0)),
            pl.BlockSpec(memory_space=pl.ANY),
        ],
        scratch_shapes=[
            pltpu.VMEM((2, 32, 4, 8, NZ), f32),
            pltpu.VMEM((2, 2, 128), f32),
            pltpu.SemaphoreType.DMA((4,)),
        ],
        compiler_params=pltpu.CompilerParams(vmem_limit_bytes=60 * 2**20),
        cost_estimate=pl.CostEstimate(flops=1000, bytes_accessed=1000, transcendentals=0),
        name="margin_shares",
    )(place, kept, across, straight, skew, orbitals)


def moved(array, axes, step):
    size = lax.axis_size(axes)
    return lax.ppermute(array, axes, [(i, (i + step) % size) for i in range(size)])


def pick(array, index):
    return lax.dynamic_index_in_dim(array, index, 0, keepdims=False)


def shifted(array, axes, destination):
    sizes = [lax.axis_size(name) for name in axes]
    pairs = []
    for index in np.ndindex(*sizes):
        goal = destination(*index)
        pairs.append((int(np.ravel_multi_index(index, sizes)), int(np.ravel_multi_index(goal, sizes))))
    return lax.ppermute(array, axes, pairs)


def after(array, other):
    return array + other[(0,) * other.ndim] * 0.0


def local(orbitals, kernel):
    xh, xl, y, core = [lax.axis_index(name) for name in ("xh", "xl", "y", "core")]
    place = jnp.stack([xl, y, core, xh]).astype(jnp.int32)
    table = jnp.asarray(make_table())

    def half(array, h):
        return lax.dynamic_slice_in_dim(array, h * (NY // 2), NY // 2, 2)

    with jax.named_scope("source_slabs"):
        pieces = [pick(orbitals, y)]
        for r in range(1, 4):
            pieces.append(moved(pick(orbitals, (y + r) % 4), "y", r))

    with jax.named_scope("all_orbitals"):
        theirs = moved(half(orbitals, 1 - xh), "xh", 1)

    with jax.named_scope("target_slabs"):
        def band(i, j):
            return pick(orbitals, 2 * (xl ^ i) + (core ^ j))

        came = moved(jnp.stack([band(0, 1), band(1, 1)]), "core", 1)
        across = moved(jnp.stack([band(1, 0), came[1]]), "xl", 1)
        part = jnp.stack([jnp.stack([band(0, 0), came[0]]), across])
        part = after(after(part, pieces[2]), theirs)
        lower = moved(part, "y", 1)
        upper = moved(part, "y", -1)
        target_parts = [part, lower, moved(lower[0], "y", 1), moved(upper[1], "y", -1), upper]

    own = after(jnp.stack(pieces), across)

    with jax.named_scope("source_fields"):
        own_other = moved(own, "xl", 1)
        far = moved(own, "z", 1)
        depth = lax.axis_size("z")
        near_other = shifted(own, ("z", "xh", "xl"), lambda k, h, l: ((k + h) % depth, 1 - h, 1 - l))
        near = moved(near_other, "xl", 1)
        far_other = moved(own_other, "z", 1)
        fields = []
        for slabs, other in ((own, own_other), (near, near_other), (far, far_other)):
            fields.append([slabs, moved(slabs, "core", 1), other, moved(other, "core", 1)])

    with jax.named_scope("all_orbitals"):
        events = [*target_parts, *[part for field in fields for part in field]]
        both = both_halves(place, orbitals, theirs, *events)
        everything = lax.all_gather(both, "z", axis=0, tiled=True)

    up, down, up_second, down_second, keep = pair_terms(place, target_parts, fields, kernel, table)

    with jax.named_scope("sum_partials"):
        low = moved(up, "y", 1)
        high = moved(down, "y", -1)
        zero = keep[0] + high[1] + moved(up_second + low[0], "y", 1)
        one = keep[1] + low[1] + moved(down_second + high[0], "y", -1)

    with jax.named_scope("to_slabs"):
        came = moved(jnp.stack([zero[1], one[1]]), "core", 1)
        kept = jnp.stack([zero[0], came[0]])
        sent = jnp.stack([one[0], came[1]])
        across = moved(sent, "xl", 1)
        straight = moved(half(kept, 1 - xh), "xh", 1)
        skew = shifted(half(sent, 1 - xh), ("xh", "xl"), lambda h, l: (1 - h, 1 - l))

    with jax.named_scope("margin"):
        shares, exchange_terms = margin_shares(place, kept, across, straight, skew, everything)
        got = lax.all_to_all(shares, ("xh", "xl", "y", "core"), split_axis=0, concat_axis=0, tiled=True)
        margin = jnp.sum(got, axis=0).reshape(64, 4)
    return exchange_terms, margin


def solution(mesh):
    fine = Mesh(mesh.devices.reshape(8, 2, 2, 4, 2), ("z", "xh", "xl", "y", "core"))
    blk = ("z", "xh")
    slab = ("xl", "y", "core")
    return jax.shard_map(
        local,
        mesh=fine,
        in_specs=(P(blk, slab, None, None), P()),
        out_specs=(P(blk, slab, None, None), P(None, blk)),
        check_vma=False,
    )
```

time: 191 us -> 180 us (0.942)
  starting transfers between devices: 38 us -> 52.6 us
  waiting for transfers between devices: 64.4 us -> 51.7 us
  local copies, waits for them, and re-layouts: 12.8 us -> 6.84 us
  Pallas kernels: 41.3 us -> 35.5 us
    ppermute x23 -> x27, starting transfers between devices: 33.1 us -> 51.9 us  [moved(): lax.ppermute(array, axes, [(i, (i + step) % size) for i in range(size)])]
    ppermute x2, waiting for transfers between devices: 15.1 us -> 4.65 us  [shifted(): return lax.ppermute(array, axes, pairs)]
    pallas_call x5 -> x3, Pallas kernels: 41.3 us -> 35.5 us  [the longest x1 26.7 us: pair_terms(): pl.pallas_call(pair_kernel, out_shape=[whole, whole, piece, piece, whole]...]
    ppermute x2, starting transfers between devices: 4.83 us -> 0.63 us  [shifted(): return lax.ppermute(array, axes, pairs)]
    unnamed x35 -> x43, local copies, waits for them, and re-layouts: 7.45 us -> 3.49 us
    squeeze x2 -> x0, local copies, waits for them, and re-layouts: 2.58 us -> none  [the longest x1 1.43 us: local(): early[3]]
    ppermute x23 -> x27, waiting for transfers between devices: 49.3 us -> 47 us  [moved(): lax.ppermute(array, axes, [(i, (i + step) % size) for i in range(size)])]
  transfers between devices with their start and end apart: 26 -> 30, of which waited for: 14 -> 12; matrix products, arithmetic and copies ran while one was open for 4% -> 4% of each run, Pallas kernels for 17% -> 15%
where the time goes in v1:
time: 180 us
  starting transfers between devices  52.6 us (29%)
  waiting for transfers between devices  51.7 us (29%)
  Pallas kernels  35.5 us (20%)
  between operations  16.5 us (9%)
  blocking collectives  11.8 us (7%)
  local copies, waits for them, and re-layouts  6.84 us (4%)
  other arithmetic  4.81 us (3%)
    ppermute x27, starting transfers between devices, moved(): lax.ppermute(array, axes, [(i, (i + step) % size) for i in range(size)])  51.9 us
    ppermute x27, waiting for transfers between devices, moved(): lax.ppermute(array, axes, [(i, (i + step) % size) for i in range(size)])  47 us
    pallas_call x1, Pallas kernels, pair_terms(): pl.pallas_call(pair_kernel, out_shape=[whole, whole, piece, piece, whole]...  26.7 us
    all_to_all x1, blocking collectives, local(): lax.all_to_all(shares, ('xh', 'xl', 'y', 'core'), split_axis=0, concat_ax...  11.8 us
    pallas_call x1, Pallas kernels, margin_shares(): pl.pallas_call(margin_kernel, grid=(2,), out_shape=[jax.ShapeDtypeStruct(...  6.79 us
    ppermute x2, waiting for transfers between devices, shifted(): return lax.ppermute(array, axes, pairs)  4.65 us
  transfers between devices with their start and end apart: 30, of which 12 were waited for; matrix products, arithmetic and copies ran while one was open for 4% of the time, Pallas kernels for 15%

profile of v1, /device:TPU:1, one launch (start us, length us, event | category | flops | bytes accessed | tf_op | source)
XLA Modules:
  0.0 179.6 jit_solution(9519313500198664163)
XLA Ops:
  7.3 1.5 constant_dynamic-slice_fusion
  8.8 3.3 %collective-permute-start = (f32[2,3,48,240]{3,2,1,0:T(8,128)S(1)}, f32[2,3,48,240]{3,2,1,0:T(8,128)S(1)}, u32[]{:S(2)}, u32[]{:S(2)}) collective-permute-start(f32[2,3,48,240]{3,2,1,0:T(8,128)S(1)} %pad_maximum_fusion.2), channel_id=1, source_target_pairs={{0,1},{1,0},{2,3},{3,2},{4,5},{5,4},{6,7},{7,6},{8,9},{9,8},{10,11... | collective-permute-start | bytes 829448 | tf_op jit(solution)/shard_map/target_slabs/ppermute | solution.py:372
  13.7 2.9 %collective-permute-start.2 = (f32[3,48,240]{2,1,0:T(8,128)S(1)}, f32[3,48,240]{2,1,0:T(8,128)S(1)}, u32[]{:S(2)}, u32[]{:S(2)}) collective-permute-start(f32[3,48,240]{2,1,0:T(8,128)S(1)} %get-tuple-element.24), channel_id=1, source_target_pairs={{0,4},{2,6},{4,0},{6,2},{1,5},{3,7},{5,1},{7,3},{8,12},{10,14},{12... | collective-permute-start | bytes 414728 | tf_op jit(solution)/shard_map/source_slabs/ppermute | solution.py:372
  17.0 2.3 %collective-permute-start.9 = (f32[3,48,240]{2,1,0:T(8,128)S(1)}, f32[3,48,240]{2,1,0:T(8,128)S(1)}, u32[]{:S(2)}, u32[]{:S(2)}) collective-permute-start(f32[3,48,240]{2,1,0:T(8,128)S(1)} %get-tuple-element.29), channel_id=1, source_target_pairs={{0,6},{2,0},{4,2},{6,4},{1,7},{3,1},{5,3},{7,5},{8,14},{10,8},{12,... | collective-permute-start | bytes 414728 | tf_op jit(solution)/shard_map/source_slabs/ppermute | solution.py:372
  21.2 1.1 collective-permute-done.3.theirs
  23.5 3.5 %collective-permute-done.1 = f32[2,3,48,240]{3,2,1,0:T(8,128)S(1)} collective-permute-done((f32[2,3,48,240]{3,2,1,0:T(8,128)S(1)}, f32[2,3,48,240]{3,2,1,0:T(8,128)S(1)}, u32[]{:S(2)}, u32[]{:S(2)}) %collective-permute-start.1) | collective-permute-done | bytes 276512 | tf_op jit(solution)/shard_map/target_slabs/ppermute | solution.py:372
  28.4 2.8 %collective-permute-start.6 = (f32[2,2,3,48,240]{4,3,2,1,0:T(8,128)S(1)}, f32[2,2,3,48,240]{4,3,2,1,0:T(8,128)S(1)}, u32[]{:S(2)}, u32[]{:S(2)}) collective-permute-start(f32[2,2,3,48,240]{4,3,2,1,0:T(8,128)S(1)} %fusion.refs_3_.refs_0_), channel_id=1, source_target_pairs={{0,6},{2,0},{4,2},{6,4},{1,7},{3,1},{5,3},{7,5},{8,14},{10,8},{12,... | collective-permute-start | bytes 1658888 | tf_op jit(solution)/shard_map/target_slabs/ppermute | solution.py:372
  31.5 1.2 collective-permute-start.11
  32.8 1.6 collective-permute-start.17
  34.4 8.6 %collective-permute-done.6.refs_7_.refs_4_ = f32[2,2,3,48,240]{4,3,2,1,0:T(8,128)S(1)} collective-permute-done((f32[2,2,3,48,240]{4,3,2,1,0:T(8,128)S(1)}, f32[2,2,3,48,240]{4,3,2,1,0:T(8,128)S(1)}, u32[]{:S(2)}, u32[]{:S(2)}) %collective-permute-start.6) | collective-permute-done | bytes 552992 | tf_op jit(solution)/shard_map/target_slabs/ppermute | solution.py:372
  43.0 1.7 collective-permute-start.10
  44.7 4.6 %collective-permute-done.13.refs_14_.refs_11_ = f32[4,3,48,240]{3,2,1,0:T(8,128)S(1)} collective-permute-done((f32[4,3,48,240]{3,2,1,0:T(8,128)S(1)}, f32[4,3,48,240]{3,2,1,0:T(8,128)S(1)}, u32[]{:S(2)}, u32[]{:S(2)}) %collective-permute-start.13) | collective-permute-done | bytes 552992 | tf_op jit(solution)/shard_map/source_fields/ppermute | solution.py:385
  49.4 1.2 collective-permute-start.14
  52.3 3.9 %collective-permute-start.16 = (f32[4,3,48,240]{3,2,1,0:T(8,128)S(1)}, f32[4,3,48,240]{3,2,1,0:T(8,128)S(1)}, u32[]{:S(2)}, u32[]{:S(2)}) collective-permute-start(f32[4,3,48,240]{3,2,1,0:T(8,128)S(1)} %collective-permute-done.13.refs_14_.refs_11_), channel_id=1, source_target_pairs={{0,1},{1,0},{2,3},{3,2},{4,5},{5,4},{6,7},{7,6},{8,9},{9,8},{10,11... | collective-permute-start | bytes 1658888 | tf_op jit(solution)/shard_map/source_fields/ppermute | solution.py:372
  56.6 4.2 %collective-permute-start.12 = (f32[4,3,48,240]{3,2,1,0:T(8,128)S(1)}, f32[4,3,48,240]{3,2,1,0:T(8,128)S(1)}, u32[]{:S(2)}, u32[]{:S(2)}) collective-permute-start(f32[4,3,48,240]{3,2,1,0:T(8,128)S(1)} %collective-permute-done.11.refs_10_.refs_7_), channel_id=1, source_target_pairs={{0,1},{1,0},{2,3},{3,2},{4,5},{5,4},{6,7},{7,6},{8,9},{9,8},{10,11... | collective-permute-start | bytes 1658888 | tf_op jit(solution)/shard_map/source_fields/ppermute | solution.py:372
  60.8 2.1 %collective-permute-start.18 = (f32[4,3,48,240]{3,2,1,0:T(8,128)S(1)}, f32[4,3,48,240]{3,2,1,0:T(8,128)S(1)}, u32[]{:S(2)}, u32[]{:S(2)}) collective-permute-start(f32[4,3,48,240]{3,2,1,0:T(8,128)S(1)} %collective-permute-done.17.refs_16_.refs_13_), channel_id=1, source_target_pairs={{0,1},{1,0},{2,3},{3,2},{4,5},{5,4},{6,7},{7,6},{8,9},{9,8},{10,11... | collective-permute-start | bytes 1658888 | tf_op jit(solution)/shard_map/source_fields/ppermute | solution.py:372
  62.9 2.3 %collective-permute-start.15 = (f32[4,3,48,240]{3,2,1,0:T(8,128)S(1)}, f32[4,3,48,240]{3,2,1,0:T(8,128)S(1)}, u32[]{:S(2)}, u32[]{:S(2)}) collective-permute-start(f32[4,3,48,240]{3,2,1,0:T(8,128)S(1)} %collective-permute-done.14.refs_12_.refs_9_), channel_id=1, source_target_pairs={{0,1},{1,0},{2,3},{3,2},{4,5},{5,4},{6,7},{7,6},{8,9},{9,8},{10,11... | collective-permute-start | bytes 1658888 | tf_op jit(solution)/shard_map/source_fields/ppermute | solution.py:372
  65.1 2.4 %collective-permute-start.20 = (f32[4,3,48,240]{3,2,1,0:T(8,128)S(1)}, f32[4,3,48,240]{3,2,1,0:T(8,128)}, u32[]{:S(2)}, u32[]{:S(2)}) collective-permute-start(f32[4,3,48,240]{3,2,1,0:T(8,128)S(1)} %collective-permute-done.19.refs_18_.refs_15_), channel_id=1, source_target_pairs={{0,1},{1,0},{2,3},{3,2},{4,5},{5,4},{6,7},{7,6},{8,9},{9,8},{10,11... | collective-permute-start | bytes 1658888 | tf_op jit(solution)/shard_map/source_fields/ppermute | solution.py:372
  70.3 2.0 %both_halves.1 = f32[8,3,24,240]{3,2,1,0:T(8,128)} custom-call(s32[4]{0:T(128)} %pad_add_fusion.refs_0_.place, f32[4,3,48,240]{3,2,1,0:T(8,128)} %orbitals.1, f32[4,3,24,240]{3,2,1,0:T(8,128)} %copy-done.17, f32[2,2,3,48,240]{4,3,2,1,0:T(8,128)} %copy-done.2, f32[2,2,3,48,240]{4,3,2,1,0:T(8,128)} %copy-done.4, f32[2,3,48,240]{3,2,1,0:T(8,128)} %copy-done.16, ...), custom_call_target="tpu_custom_call" | custom-call | flops 1000 | bytes 1000 | tf_op jit(solution)/shard_map/all_orbitals/both_halves/pallas_call | solution.py:276
  72.4 26.7 %pair_terms.1 = (f32[2,2,3,48,240]{4,3,2,1,0:T(8,128)}, f32[2,2,3,48,240]{4,3,2,1,0:T(8,128)}, f32[2,3,48,240]{3,2,1,0:T(8,128)}, f32[2,3,48,240]{3,2,1,0:T(8,128)}, f32[2,2,3,48,240]{4,3,2,1,0:T(8,128)}) custom-call(s32[4]{0:T(128)} %pad_add_fusion.refs_0_.place, bf16[1248,768]{1,0:T(8,128)(2,1)} %constant.73.clone.refs_1_, f32[48,48,240]{2,1,0:T(8,128)} %refs_2_.1, ...), custom_call_target="tpu_custom_call" | custom-call | flops 1000 | bytes 1000 | tf_op jit(solution)/shard_map/pair_terms/pallas_call | solution.py:237
  99.0 1.7 collective-permute-start.21
  100.7 13.6 %collective-permute-done.21 = f32[2,2,3,48,240]{4,3,2,1,0:T(8,128)S(1)} collective-permute-done((f32[2,2,3,48,240]{4,3,2,1,0:T(8,128)}, f32[2,2,3,48,240]{4,3,2,1,0:T(8,128)S(1)}, u32[]{:S(2)}, u32[]{:S(2)}) %collective-permute-start.21) | collective-permute-done | bytes 552992 | tf_op jit(solution)/shard_map/sum_partials/ppermute | solution.py:372
  115.3 2.9 %collective-permute-start.24 = (f32[2,3,48,240]{3,2,1,0:T(8,128)S(1)}, f32[2,3,48,240]{3,2,1,0:T(8,128)S(1)}, u32[]{:S(2)}, u32[]{:S(2)}) collective-permute-start(f32[2,3,48,240]{3,2,1,0:T(8,128)S(1)} %fusion.1), channel_id=1, source_target_pairs={{0,6},{2,0},{4,2},{6,4},{1,7},{3,1},{5,3},{7,5},{8,14},{10,8},{12,... | collective-permute-start | bytes 829448 | tf_op jit(solution)/shard_map/sum_partials/ppermute | solution.py:372
  119.5 4.2 %collective-permute-done.24 = f32[2,3,48,240]{3,2,1,0:T(8,128)S(1)} collective-permute-done((f32[2,3,48,240]{3,2,1,0:T(8,128)S(1)}, f32[2,3,48,240]{3,2,1,0:T(8,128)S(1)}, u32[]{:S(2)}, u32[]{:S(2)}) %collective-permute-start.24) | collective-permute-done | bytes 276512 | tf_op jit(solution)/shard_map/sum_partials/ppermute | solution.py:372
  123.8 4.5 %collective-permute-done.23 = f32[2,3,48,240]{3,2,1,0:T(8,128)S(1)} collective-permute-done((f32[2,3,48,240]{3,2,1,0:T(8,128)S(1)}, f32[2,3,48,240]{3,2,1,0:T(8,128)S(1)}, u32[]{:S(2)}, u32[]{:S(2)}) %collective-permute-start.23) | collective-permute-done | bytes 276512 | tf_op jit(solution)/shard_map/sum_partials/ppermute | solution.py:372
  128.3 1.2 fusion.6
  129.6 2.0 %collective-permute-start.25 = (f32[2,3,48,240]{3,2,1,0:T(8,128)S(1)}, f32[2,3,48,240]{3,2,1,0:T(8,128)S(1)}, u32[]{:S(2)}, u32[]{:S(2)}) collective-permute-start(f32[2,3,48,240]{3,2,1,0:T(8,128)S(1)} %pad_maximum_fusion.4), channel_id=1, source_target_pairs={{0,1},{1,0},{2,3},{3,2},{4,5},{5,4},{6,7},{7,6},{8,9},{9,8},{10,11... | collective-permute-start | bytes 829448 | tf_op jit(solution)/shard_map/to_slabs/ppermute | solution.py:372
  131.5 1.2 collective-permute-done.25
  133.2 9.3 %collective-permute-start.27 = (f32[2,3,24,240]{3,2,1,0:T(8,128)S(1)}, f32[2,3,24,240]{3,2,1,0:T(8,128)S(1)}, u32[]{:S(2)}, u32[]{:S(2)}) collective-permute-start(f32[2,3,24,240]{3,2,1,0:T(8,128)S(1)} %fusion.8), channel_id=1, source_target_pairs={{0,16},{16,0},{1,17},{17,1},{2,18},{18,2},{3,19},{19,3},{4,20},{20... | collective-permute-start | bytes 414728 | tf_op jit(solution)/shard_map/to_slabs/ppermute | solution.py:372
  143.6 9.0 %collective-permute-done.27.straight = f32[2,3,24,240]{3,2,1,0:T(8,128)S(1)} collective-permute-done((f32[2,3,24,240]{3,2,1,0:T(8,128)S(1)}, f32[2,3,24,240]{3,2,1,0:T(8,128)S(1)}, u32[]{:S(2)}, u32[]{:S(2)}) %collective-permute-start.27) | collective-permute-done | bytes 138272 | tf_op jit(solution)/shard_map/to_slabs/ppermute | solution.py:372
  153.4 6.8 %margin_shares.1 = (f32[32,1,256]{2,1,0:T(1,128)}, f32[4,3,48,240]{3,2,1,0:T(8,128)}) custom-call(s32[4]{0:T(128)} %pad_add_fusion.refs_0_.place, f32[2,3,48,240]{3,2,1,0:T(8,128)} %pad_maximum_fusion.kept, f32[2,3,48,240]{3,2,1,0:T(8,128)} %copy-done.18, f32[2,3,24,240]{3,2,1,0:T(8,128)} %copy-done.19, f32[2,3,24,240]{3,2,1,0:T(8,128)} %copy-done.20, ...), custom_call_target="tpu_custom_call" | custom-call | flops 1000 | bytes 1000 | tf_op jit(solution)/shard_map/margin/margin_shares/pallas_call | solution.py:345
  160.2 11.8 %all_to_all.5 = f32[32,1,256]{2,1,0:T(1,128)S(1)} all-to-all(f32[32,1,256]{2,1,0:T(1,128)} %get-tuple-element.15), channel_id=1, replica_groups=mesh['z'=8,'xh'=2,'xl'=2,'y'=4,'core'=2] {'xh','xl','y','core'}, dimensions={0} | all-to-all | bytes 65536 | tf_op jit(solution)/shard_map/margin/all_to_all | solution.py:456
  (102 shorter events, 15.1 us)
Async XLA Ops:
  7.2 145.5 %all-gather.2.cloned.1.call-start = ((), (), s32[]{:S(2)}) async-start(), calls=%async_computation.1 | async-start | bytes 5308416 | tf_op jit(solution)/shard_map/all_orbitals/all_gather | solution.py:436
  8.8 4.5 %collective-permute-start = (f32[2,3,48,240]{3,2,1,0:T(8,128)S(1)}, f32[2,3,48,240]{3,2,1,0:T(8,128)S(1)}, u32[]{:S(2)}, u32[]{:S(2)}) collective-permute-start(f32[2,3,48,240]{3,2,1,0:T(8,128)S(1)} %pad_maximum_fusion.2), channel_id=1, source_target_pairs={{0,1},{1,0},{2,3},{3,2},{4,5},{5,4},{6,7},{7,6},{8,9},{9,8},{10,11... | collective-permute-start | bytes 829448 | tf_op jit(solution)/shard_map/target_slabs/ppermute | solution.py:372
  12.1 10.2 %collective-permute-start.3 = (f32[4,3,24,240]{3,2,1,0:T(8,128)S(1)}, f32[4,3,24,240]{3,2,1,0:T(8,128)S(1)}, u32[]{:S(2)}, u32[]{:S(2)}) collective-permute-start(f32[4,3,24,240]{3,2,1,0:T(8,128)S(1)} %constant_dynamic-slice_fusion.1), channel_id=1, source_target_pairs={{0,16},{16,0},{1,17},{17,1},{2,18},{18,2},{3,19},{19,3},{4,20},{20... | collective-permute-start | bytes 829448 | tf_op jit(solution)/shard_map/all_orbitals/ppermute | solution.py:372
  13.4 13.6 %collective-permute-start.1 = (f32[2,3,48,240]{3,2,1,0:T(8,128)S(1)}, f32[2,3,48,240]{3,2,1,0:T(8,128)S(1)}, u32[]{:S(2)}, u32[]{:S(2)}) collective-permute-start(f32[2,3,48,240]{3,2,1,0:T(8,128)S(1)} %pad_maximum_fusion.3), channel_id=1, source_target_pairs={{0,8},{8,0},{1,9},{9,1},{2,10},{10,2},{3,11},{11,3},{4,12},{12,4},... | collective-permute-start | bytes 829448 | tf_op jit(solution)/shard_map/target_slabs/ppermute | solution.py:372
  13.7 6.3 %collective-permute-start.2 = (f32[3,48,240]{2,1,0:T(8,128)S(1)}, f32[3,48,240]{2,1,0:T(8,128)S(1)}, u32[]{:S(2)}, u32[]{:S(2)}) collective-permute-start(f32[3,48,240]{2,1,0:T(8,128)S(1)} %get-tuple-element.24), channel_id=1, source_target_pairs={{0,4},{2,6},{4,0},{6,2},{1,5},{3,7},{5,1},{7,3},{8,12},{10,14},{12... | collective-permute-start | bytes 414728 | tf_op jit(solution)/shard_map/source_slabs/ppermute | solution.py:372
  16.6 14.6 %collective-permute-start.8 = (f32[3,48,240]{2,1,0:T(8,128)S(1)}, f32[3,48,240]{2,1,0:T(8,128)S(1)}, u32[]{:S(2)}, u32[]{:S(2)}) collective-permute-start(f32[3,48,240]{2,1,0:T(8,128)S(1)} %get-tuple-element.23), channel_id=1, source_target_pairs={{0,2},{2,4},{4,6},{6,0},{1,3},{3,5},{5,7},{7,1},{8,10},{10,12},{12... | collective-permute-start | bytes 414728 | tf_op jit(solution)/shard_map/source_slabs/ppermute | solution.py:372
  17.0 14.2 %collective-permute-start.9 = (f32[3,48,240]{2,1,0:T(8,128)S(1)}, f32[3,48,240]{2,1,0:T(8,128)S(1)}, u32[]{:S(2)}, u32[]{:S(2)}) collective-permute-start(f32[3,48,240]{2,1,0:T(8,128)S(1)} %get-tuple-element.29), channel_id=1, source_target_pairs={{0,6},{2,0},{4,2},{6,4},{1,7},{3,1},{5,3},{7,5},{8,14},{10,8},{12,... | collective-permute-start | bytes 414728 | tf_op jit(solution)/shard_map/source_slabs/ppermute | solution.py:372
  28.4 41.9 %copy-start.2 = (f32[2,2,3,48,240]{4,3,2,1,0:T(8,128)}, f32[2,2,3,48,240]{4,3,2,1,0:T(8,128)S(1)}, u32[]{:S(2)}) copy-start(f32[2,2,3,48,240]{4,3,2,1,0:T(8,128)S(1)} %fusion.refs_3_.refs_0_) | copy-start | bytes 1658884
  28.4 14.6 %collective-permute-start.6 = (f32[2,2,3,48,240]{4,3,2,1,0:T(8,128)S(1)}, f32[2,2,3,48,240]{4,3,2,1,0:T(8,128)S(1)}, u32[]{:S(2)}, u32[]{:S(2)}) collective-permute-start(f32[2,2,3,48,240]{4,3,2,1,0:T(8,128)S(1)} %fusion.refs_3_.refs_0_), channel_id=1, source_target_pairs={{0,6},{2,0},{4,2},{6,4},{1,7},{3,1},{5,3},{7,5},{8,14},{10,8},{12,... | collective-permute-start | bytes 1658888 | tf_op jit(solution)/shard_map/target_slabs/ppermute | solution.py:372
  31.3 39.0 %copy-start.1 = (f32[4,3,48,240]{3,2,1,0:T(8,128)}, f32[4,3,48,240]{3,2,1,0:T(8,128)S(1)}, u32[]{:S(2)}) copy-start(f32[4,3,48,240]{3,2,1,0:T(8,128)S(1)} %maximum_add_fusion.1.refs_8_.refs_5_) | copy-start | bytes 1658884
  31.3 18.1 %collective-permute-start.13 = (f32[4,3,48,240]{3,2,1,0:T(8,128)S(1)}, f32[4,3,48,240]{3,2,1,0:T(8,128)S(1)}, u32[]{:S(2)}, u32[]{:S(2)}) collective-permute-start(f32[4,3,48,240]{3,2,1,0:T(8,128)S(1)} %maximum_add_fusion.1.refs_8_.refs_5_), channel_id=1, source_target_pairs={{0,24},{8,16},{16,40},{24,32},{32,56},{40,48},{48,72},{56,64},{64,... | collective-permute-start | bytes 1658888 | tf_op jit(solution)/shard_map/source_fields/ppermute | solution.py:385
  31.5 19.1 %collective-permute-start.11 = (f32[4,3,48,240]{3,2,1,0:T(8,128)S(1)}, f32[4,3,48,240]{3,2,1,0:T(8,128)S(1)}, u32[]{:S(2)}, u32[]{:S(2)}) collective-permute-start(f32[4,3,48,240]{3,2,1,0:T(8,128)S(1)} %maximum_add_fusion.1.refs_8_.refs_5_), channel_id=1, source_target_pairs={{0,8},{8,0},{1,9},{9,1},{2,10},{10,2},{3,11},{11,3},{4,12},{12,4},... | collective-permute-start | bytes 1658888 | tf_op jit(solution)/shard_map/source_fields/ppermute | solution.py:372
  32.7 17.9 %collective-permute-start.4 = (f32[2,2,3,48,240]{4,3,2,1,0:T(8,128)S(1)}, f32[2,2,3,48,240]{4,3,2,1,0:T(8,128)S(1)}, u32[]{:S(2)}, u32[]{:S(2)}) collective-permute-start(f32[2,2,3,48,240]{4,3,2,1,0:T(8,128)S(1)} %fusion.refs_3_.refs_0_), channel_id=1, source_target_pairs={{0,2},{2,4},{4,6},{6,0},{1,3},{3,5},{5,7},{7,1},{8,10},{10,12},{12... | collective-permute-start | bytes 1658888 | tf_op jit(solution)/shard_map/target_slabs/ppermute | solution.py:372
  32.8 18.5 %collective-permute-start.17 = (f32[4,3,48,240]{3,2,1,0:T(8,128)S(1)}, f32[4,3,48,240]{3,2,1,0:T(8,128)S(1)}, u32[]{:S(2)}, u32[]{:S(2)}) collective-permute-start(f32[4,3,48,240]{3,2,1,0:T(8,128)S(1)} %maximum_add_fusion.1.refs_8_.refs_5_), channel_id=1, source_target_pairs={{0,32},{32,64},{64,96},{96,128},{128,160},{160,192},{192,224},{224... | collective-permute-start | bytes 1658888 | tf_op jit(solution)/shard_map/source_fields/ppermute | solution.py:372
  43.0 9.3 %collective-permute-start.10 = (f32[4,3,48,240]{3,2,1,0:T(8,128)S(1)}, f32[4,3,48,240]{3,2,1,0:T(8,128)S(1)}, u32[]{:S(2)}, u32[]{:S(2)}) collective-permute-start(f32[4,3,48,240]{3,2,1,0:T(8,128)S(1)} %maximum_add_fusion.1.refs_8_.refs_5_), channel_id=1, source_target_pairs={{0,1},{1,0},{2,3},{3,2},{4,5},{5,4},{6,7},{7,6},{8,9},{9,8},{10,11... | collective-permute-start | bytes 1658888 | tf_op jit(solution)/shard_map/source_fields/ppermute | solution.py:372
  49.4 13.5 %collective-permute-start.14 = (f32[4,3,48,240]{3,2,1,0:T(8,128)S(1)}, f32[4,3,48,240]{3,2,1,0:T(8,128)S(1)}, u32[]{:S(2)}, u32[]{:S(2)}) collective-permute-start(f32[4,3,48,240]{3,2,1,0:T(8,128)S(1)} %collective-permute-done.13.refs_14_.refs_11_), channel_id=1, source_target_pairs={{0,8},{8,0},{1,9},{9,1},{2,10},{10,2},{3,11},{11,3},{4,12},{12,4},... | collective-permute-start | bytes 1658888 | tf_op jit(solution)/shard_map/source_fields/ppermute | solution.py:372
  50.6 14.5 %collective-permute-start.19 = (f32[4,3,48,240]{3,2,1,0:T(8,128)S(1)}, f32[4,3,48,240]{3,2,1,0:T(8,128)S(1)}, u32[]{:S(2)}, u32[]{:S(2)}) collective-permute-start(f32[4,3,48,240]{3,2,1,0:T(8,128)S(1)} %collective-permute-done.11.refs_10_.refs_7_), channel_id=1, source_target_pairs={{0,32},{32,64},{64,96},{96,128},{128,160},{160,192},{192,224},{224... | collective-permute-start | bytes 1658888 | tf_op jit(solution)/shard_map/source_fields/ppermute | solution.py:372
  50.7 5.9 %collective-permute-start.7 = (f32[2,3,48,240]{3,2,1,0:T(8,128)S(1)}, f32[2,3,48,240]{3,2,1,0:T(8,128)S(1)}, u32[]{:S(2)}, u32[]{:S(2)}) collective-permute-start(f32[2,3,48,240]{3,2,1,0:T(8,128)S(1)} %slice_bitcast_fusion.2), channel_id=1, source_target_pairs={{0,6},{2,0},{4,2},{6,4},{1,7},{3,1},{5,3},{7,5},{8,14},{10,8},{12,... | collective-permute-start | bytes 829448 | tf_op jit(solution)/shard_map/target_slabs/ppermute | solution.py:372
  51.2 9.5 %collective-permute-start.5 = (f32[2,3,48,240]{3,2,1,0:T(8,128)S(1)}, f32[2,3,48,240]{3,2,1,0:T(8,128)S(1)}, u32[]{:S(2)}, u32[]{:S(2)}) collective-permute-start(f32[2,3,48,240]{3,2,1,0:T(8,128)S(1)} %slice_bitcast_fusion.3), channel_id=1, source_target_pairs={{0,2},{2,4},{4,6},{6,0},{1,3},{3,5},{5,7},{7,1},{8,10},{10,12},{12... | collective-permute-start | bytes 829448 | tf_op jit(solution)/shard_map/target_slabs/ppermute | solution.py:372
  52.3 15.8 %collective-permute-start.16 = (f32[4,3,48,240]{3,2,1,0:T(8,128)S(1)}, f32[4,3,48,240]{3,2,1,0:T(8,128)S(1)}, u32[]{:S(2)}, u32[]{:S(2)}) collective-permute-start(f32[4,3,48,240]{3,2,1,0:T(8,128)S(1)} %collective-permute-done.13.refs_14_.refs_11_), channel_id=1, source_target_pairs={{0,1},{1,0},{2,3},{3,2},{4,5},{5,4},{6,7},{7,6},{8,9},{9,8},{10,11... | collective-permute-start | bytes 1658888 | tf_op jit(solution)/shard_map/source_fields/ppermute | solution.py:372
  56.6 11.6 %collective-permute-start.12 = (f32[4,3,48,240]{3,2,1,0:T(8,128)S(1)}, f32[4,3,48,240]{3,2,1,0:T(8,128)S(1)}, u32[]{:S(2)}, u32[]{:S(2)}) collective-permute-start(f32[4,3,48,240]{3,2,1,0:T(8,128)S(1)} %collective-permute-done.11.refs_10_.refs_7_), channel_id=1, source_target_pairs={{0,1},{1,0},{2,3},{3,2},{4,5},{5,4},{6,7},{7,6},{8,9},{9,8},{10,11... | collective-permute-start | bytes 1658888 | tf_op jit(solution)/shard_map/source_fields/ppermute | solution.py:372
  60.8 7.4 %collective-permute-start.18 = (f32[4,3,48,240]{3,2,1,0:T(8,128)S(1)}, f32[4,3,48,240]{3,2,1,0:T(8,128)S(1)}, u32[]{:S(2)}, u32[]{:S(2)}) collective-permute-start(f32[4,3,48,240]{3,2,1,0:T(8,128)S(1)} %collective-permute-done.17.refs_16_.refs_13_), channel_id=1, source_target_pairs={{0,1},{1,0},{2,3},{3,2},{4,5},{5,4},{6,7},{7,6},{8,9},{9,8},{10,11... | collective-permute-start | bytes 1658888 | tf_op jit(solution)/shard_map/source_fields/ppermute | solution.py:372
  62.9 5.3 %collective-permute-start.15 = (f32[4,3,48,240]{3,2,1,0:T(8,128)S(1)}, f32[4,3,48,240]{3,2,1,0:T(8,128)S(1)}, u32[]{:S(2)}, u32[]{:S(2)}) collective-permute-start(f32[4,3,48,240]{3,2,1,0:T(8,128)S(1)} %collective-permute-done.14.refs_12_.refs_9_), channel_id=1, source_target_pairs={{0,1},{1,0},{2,3},{3,2},{4,5},{5,4},{6,7},{7,6},{8,9},{9,8},{10,11... | collective-permute-start | bytes 1658888 | tf_op jit(solution)/shard_map/source_fields/ppermute | solution.py:372
  65.1 5.1 %collective-permute-start.20 = (f32[4,3,48,240]{3,2,1,0:T(8,128)S(1)}, f32[4,3,48,240]{3,2,1,0:T(8,128)}, u32[]{:S(2)}, u32[]{:S(2)}) collective-permute-start(f32[4,3,48,240]{3,2,1,0:T(8,128)S(1)} %collective-permute-done.19.refs_18_.refs_15_), channel_id=1, source_target_pairs={{0,1},{1,0},{2,3},{3,2},{4,5},{5,4},{6,7},{7,6},{8,9},{9,8},{10,11... | collective-permute-start | bytes 1658888 | tf_op jit(solution)/shard_map/source_fields/ppermute | solution.py:372
  99.0 15.3 %collective-permute-start.21 = (f32[2,2,3,48,240]{4,3,2,1,0:T(8,128)}, f32[2,2,3,48,240]{4,3,2,1,0:T(8,128)S(1)}, u32[]{:S(2)}, u32[]{:S(2)}) collective-permute-start(f32[2,2,3,48,240]{4,3,2,1,0:T(8,128)} %get-tuple-element.10), channel_id=1, source_target_pairs={{0,6},{2,0},{4,2},{6,4},{1,7},{3,1},{5,3},{7,5},{8,14},{10,8},{12,... | collective-permute-start | bytes 1658888 | tf_op jit(solution)/shard_map/sum_partials/ppermute | solution.py:372
  100.7 17.5 %collective-permute-start.22 = (f32[2,2,3,48,240]{4,3,2,1,0:T(8,128)}, f32[2,2,3,48,240]{4,3,2,1,0:T(8,128)S(1)}, u32[]{:S(2)}, u32[]{:S(2)}) collective-permute-start(f32[2,2,3,48,240]{4,3,2,1,0:T(8,128)} %get-tuple-element.12), channel_id=1, source_target_pairs={{0,2},{2,4},{4,6},{6,0},{1,3},{3,5},{5,7},{7,1},{8,10},{10,12},{12... | collective-permute-start | bytes 1658888 | tf_op jit(solution)/shard_map/sum_partials/ppermute | solution.py:372
  115.3 8.5 %collective-permute-start.24 = (f32[2,3,48,240]{3,2,1,0:T(8,128)S(1)}, f32[2,3,48,240]{3,2,1,0:T(8,128)S(1)}, u32[]{:S(2)}, u32[]{:S(2)}) collective-permute-start(f32[2,3,48,240]{3,2,1,0:T(8,128)S(1)} %fusion.1), channel_id=1, source_target_pairs={{0,6},{2,0},{4,2},{6,4},{1,7},{3,1},{5,3},{7,5},{8,14},{10,8},{12,... | collective-permute-start | bytes 829448 | tf_op jit(solution)/shard_map/sum_partials/ppermute | solution.py:372
  119.2 9.1 %collective-permute-start.23 = (f32[2,3,48,240]{3,2,1,0:T(8,128)S(1)}, f32[2,3,48,240]{3,2,1,0:T(8,128)S(1)}, u32[]{:S(2)}, u32[]{:S(2)}) collective-permute-start(f32[2,3,48,240]{3,2,1,0:T(8,128)S(1)} %fusion.4), channel_id=1, source_target_pairs={{0,2},{2,4},{4,6},{6,0},{1,3},{3,5},{5,7},{7,1},{8,10},{10,12},{12... | collective-permute-start | bytes 829448 | tf_op jit(solution)/shard_map/sum_partials/ppermute | solution.py:372
  129.6 3.2 %collective-permute-start.25 = (f32[2,3,48,240]{3,2,1,0:T(8,128)S(1)}, f32[2,3,48,240]{3,2,1,0:T(8,128)S(1)}, u32[]{:S(2)}, u32[]{:S(2)}) collective-permute-start(f32[2,3,48,240]{3,2,1,0:T(8,128)S(1)} %pad_maximum_fusion.4), channel_id=1, source_target_pairs={{0,1},{1,0},{2,3},{3,2},{4,5},{5,4},{6,7},{7,6},{8,9},{9,8},{10,11... | collective-permute-start | bytes 829448 | tf_op jit(solution)/shard_map/to_slabs/ppermute | solution.py:372
  132.8 19.8 %collective-permute-start.26 = (f32[2,3,48,240]{3,2,1,0:T(8,128)S(1)}, f32[2,3,48,240]{3,2,1,0:T(8,128)S(1)}, u32[]{:S(2)}, u32[]{:S(2)}) collective-permute-start(f32[2,3,48,240]{3,2,1,0:T(8,128)S(1)} %pad_maximum_fusion.1), channel_id=1, source_target_pairs={{0,8},{8,0},{1,9},{9,1},{2,10},{10,2},{3,11},{11,3},{4,12},{12,4},... | collective-permute-start | bytes 829448 | tf_op jit(solution)/shard_map/to_slabs/ppermute | solution.py:372
  133.2 19.4 %collective-permute-start.27 = (f32[2,3,24,240]{3,2,1,0:T(8,128)S(1)}, f32[2,3,24,240]{3,2,1,0:T(8,128)S(1)}, u32[]{:S(2)}, u32[]{:S(2)}) collective-permute-start(f32[2,3,24,240]{3,2,1,0:T(8,128)S(1)} %fusion.8), channel_id=1, source_target_pairs={{0,16},{16,0},{1,17},{17,1},{2,18},{18,2},{3,19},{19,3},{4,20},{20... | collective-permute-start | bytes 414728 | tf_op jit(solution)/shard_map/to_slabs/ppermute | solution.py:372
  142.5 10.1 %collective-permute-start.28 = (f32[2,3,24,240]{3,2,1,0:T(8,128)S(1)}, f32[2,3,24,240]{3,2,1,0:T(8,128)S(1)}, u32[]{:S(2)}, u32[]{:S(2)}) collective-permute-start(f32[2,3,24,240]{3,2,1,0:T(8,128)S(1)} %fusion.7), channel_id=1, source_target_pairs={{0,24},{8,16},{16,8},{24,0},{1,25},{9,17},{17,9},{25,1},{2,26},{10... | collective-permute-start | bytes 414728 | tf_op jit(solution)/shard_map/to_slabs/ppermute | solution.py:385
  (19 other events, 163.9 us)
Sparse Core Ops, SparseCore 0:
  72.5 65.6 all-gather.1

commit v2 on v1

--- a/solution.py
+++ b/solution.py
@@ -285,6 +285,24 @@
     )(place, orbitals, theirs, *events)
 
 
+def held_kernel(*refs):
+    del refs
+
+
+def held_until(array, *events):
+    hbm = pl.BlockSpec(memory_space=pl.ANY)
+    return pl.pallas_call(
+        held_kernel,
+        out_shape=jax.ShapeDtypeStruct(array.shape, array.dtype),
+        in_specs=[hbm] * (1 + len(events)),
+        out_specs=hbm,
+        input_output_aliases={0: 0},
+        compiler_params=pltpu.CompilerParams(vmem_limit_bytes=60 * 2**20),
+        cost_estimate=pl.CostEstimate(flops=1000, bytes_accessed=1000, transcendentals=0),
+        name="held_until",
+    )(array, *events)
+
+
 def margin_kernel(place, kept, across, straight, skew, orbitals, shares, exchange, sums, lines, sems):
     here = 2 * place[0] + place[2]
     xh = place[3]
@@ -404,6 +422,7 @@
 
     with jax.named_scope("all_orbitals"):
         theirs = moved(half(orbitals, 1 - xh), "xh", 1)
+        both = both_halves(place, orbitals, theirs)
 
     with jax.named_scope("target_slabs"):
         def band(i, j):
@@ -412,7 +431,7 @@
         came = moved(jnp.stack([band(0, 1), band(1, 1)]), "core", 1)
         across = moved(jnp.stack([band(1, 0), came[1]]), "xl", 1)
         part = jnp.stack([jnp.stack([band(0, 0), came[0]]), across])
-        part = after(after(part, pieces[2]), theirs)
+        part = after(after(part, pieces[2]), both)
         lower = moved(part, "y", 1)
         upper = moved(part, "y", -1)
         target_parts = [part, lower, moved(lower[0], "y", 1), moved(upper[1], "y", -1), upper]
@@ -432,8 +451,7 @@
 
     with jax.named_scope("all_orbitals"):
         events = [*target_parts, *[part for field in fields for part in field]]
-        both = both_halves(place, orbitals, theirs, *events)
-        everything = lax.all_gather(both, "z", axis=0, tiled=True)
+        everything = lax.all_gather(held_until(both, *events), "z", axis=0, tiled=True)
 
     up, down, up_second, down_second, keep = pair_terms(place, target_parts, fields, kernel, table)
 

time: 180 us -> 177 us (0.983)
  waiting for transfers between devices: 51.7 us -> 46.5 us
    ppermute x27, waiting for transfers between devices: 47 us -> 42.4 us  [moved(): lax.ppermute(array, axes, [(i, (i + step) % size) for i in range(size)])]
    unnamed x43 -> x41, local copies, waits for them, and re-layouts: 3.49 us -> 4.19 us
  transfers between devices with their start and end apart: 30 -> 30, of which waited for: 12 -> 11; matrix products, arithmetic and copies ran while one was open for 4% -> 4% of each run, Pallas kernels for 15% -> 16%
where the time goes in v2:
time: 177 us
  starting transfers between devices  53.4 us (30%)
  waiting for transfers between devices  46.5 us (26%)
  Pallas kernels  35.4 us (20%)
  between operations  16.5 us (9%)
  blocking collectives  12.1 us (7%)
  local copies, waits for them, and re-layouts  8.18 us (5%)
  other arithmetic  4.84 us (3%)
    ppermute x27, starting transfers between devices, moved(): lax.ppermute(array, axes, [(i, (i + step) % size) for i in range(size)])  52.4 us
    ppermute x27, waiting for transfers between devices, moved(): lax.ppermute(array, axes, [(i, (i + step) % size) for i in range(size)])  42.4 us
    pallas_call x1, Pallas kernels, pair_terms(): pl.pallas_call(pair_kernel, out_shape=[whole, whole, piece, piece, whole]...  26.7 us
    all_to_all x1, blocking collectives, local(): lax.all_to_all(shares, ('xh', 'xl', 'y', 'core'), split_axis=0, concat_ax...  12.1 us
    pallas_call x1, Pallas kernels, margin_shares(): pl.pallas_call(margin_kernel, grid=(2,), out_shape=[jax.ShapeDtypeStruct(...  6.78 us
    unnamed x41, local copies, waits for them, and re-layouts  4.19 us
    ppermute x2, waiting for transfers between devices, shifted(): return lax.ppermute(array, axes, pairs)  4.1 us
  transfers between devices with their start and end apart: 30, of which 11 were waited for; matrix products, arithmetic and copies ran while one was open for 4% of the time, Pallas kernels for 16%

profile of v2, /device:TPU:1, one launch (start us, length us, event | category | flops | bytes accessed | tf_op | source)
XLA Modules:
  0.0 176.9 jit_solution(17244385157610670952)
XLA Ops:
  7.3 1.5 constant_dynamic-slice_fusion
  8.8 3.3 %collective-permute-start = (f32[2,3,48,240]{3,2,1,0:T(8,128)S(1)}, f32[2,3,48,240]{3,2,1,0:T(8,128)S(1)}, u32[]{:S(2)}, u32[]{:S(2)}) collective-permute-start(f32[2,3,48,240]{3,2,1,0:T(8,128)S(1)} %pad_maximum_fusion.2), channel_id=1, source_target_pairs={{0,1},{1,0},{2,3},{3,2},{4,5},{5,4},{6,7},{7,6},{8,9},{9,8},{10,11... | collective-permute-start | bytes 829448 | tf_op jit(solution)/shard_map/target_slabs/ppermute | solution.py:390
  12.1 1.1 collective-permute-start.3
  13.7 2.9 %collective-permute-start.2 = (f32[3,48,240]{2,1,0:T(8,128)S(1)}, f32[3,48,240]{2,1,0:T(8,128)S(1)}, u32[]{:S(2)}, u32[]{:S(2)}) collective-permute-start(f32[3,48,240]{2,1,0:T(8,128)S(1)} %get-tuple-element.23), channel_id=1, source_target_pairs={{0,4},{2,6},{4,0},{6,2},{1,5},{3,7},{5,1},{7,3},{8,12},{10,14},{12... | collective-permute-start | bytes 414728 | tf_op jit(solution)/shard_map/source_slabs/ppermute | solution.py:390
  18.7 1.3 collective-permute-done.2
  21.2 1.1 collective-permute-done.3.theirs
  23.0 2.0 %both_halves.1.refs_0_ = f32[8,3,24,240]{3,2,1,0:T(8,128)} custom-call(s32[4]{0:T(128)} %pad_add_fusion.place.refs_0_, f32[4,3,48,240]{3,2,1,0:T(8,128)} %orbitals.1, f32[4,3,24,240]{3,2,1,0:T(8,128)} %copy-done.17), custom_call_target="tpu_custom_call" | custom-call | flops 1000 | bytes 1000 | tf_op jit(solution)/shard_map/all_orbitals/both_halves/pallas_call | solution.py:276
  25.0 1.2 slice.79
  28.3 2.8 %collective-permute-start.6 = (f32[2,2,3,48,240]{4,3,2,1,0:T(8,128)S(1)}, f32[2,2,3,48,240]{4,3,2,1,0:T(8,128)S(1)}, u32[]{:S(2)}, u32[]{:S(2)}) collective-permute-start(f32[2,2,3,48,240]{4,3,2,1,0:T(8,128)S(1)} %fusion.refs_3_.refs_1_), channel_id=1, source_target_pairs={{0,6},{2,0},{4,2},{6,4},{1,7},{3,1},{5,3},{7,5},{8,14},{10,8},{12,... | collective-permute-start | bytes 1658888 | tf_op jit(solution)/shard_map/target_slabs/ppermute | solution.py:390
  32.7 1.6 collective-permute-start.17
  34.3 8.1 %collective-permute-done.6.refs_7_.refs_5_ = f32[2,2,3,48,240]{4,3,2,1,0:T(8,128)S(1)} collective-permute-done((f32[2,2,3,48,240]{4,3,2,1,0:T(8,128)S(1)}, f32[2,2,3,48,240]{4,3,2,1,0:T(8,128)S(1)}, u32[]{:S(2)}, u32[]{:S(2)}) %collective-permute-start.6) | collective-permute-done | bytes 552992 | tf_op jit(solution)/shard_map/target_slabs/ppermute | solution.py:390
  42.5 2.2 %collective-permute-start.10 = (f32[4,3,48,240]{3,2,1,0:T(8,128)S(1)}, f32[4,3,48,240]{3,2,1,0:T(8,128)S(1)}, u32[]{:S(2)}, u32[]{:S(2)}) collective-permute-start(f32[4,3,48,240]{3,2,1,0:T(8,128)S(1)} %maximum_add_fusion.1.refs_8_.refs_6_), channel_id=1, source_target_pairs={{0,1},{1,0},{2,3},{3,2},{4,5},{5,4},{6,7},{7,6},{8,9},{9,8},{10,11... | collective-permute-start | bytes 1658888 | tf_op jit(solution)/shard_map/source_fields/ppermute | solution.py:390
  44.7 4.1 %collective-permute-done.13.refs_14_.refs_12_ = f32[4,3,48,240]{3,2,1,0:T(8,128)S(1)} collective-permute-done((f32[4,3,48,240]{3,2,1,0:T(8,128)S(1)}, f32[4,3,48,240]{3,2,1,0:T(8,128)S(1)}, u32[]{:S(2)}, u32[]{:S(2)}) %collective-permute-start.13) | collective-permute-done | bytes 552992 | tf_op jit(solution)/shard_map/source_fields/ppermute | solution.py:403
  48.8 1.3 collective-permute-start.14
  51.8 4.9 %collective-permute-start.16 = (f32[4,3,48,240]{3,2,1,0:T(8,128)S(1)}, f32[4,3,48,240]{3,2,1,0:T(8,128)S(1)}, u32[]{:S(2)}, u32[]{:S(2)}) collective-permute-start(f32[4,3,48,240]{3,2,1,0:T(8,128)S(1)} %collective-permute-done.13.refs_14_.refs_12_), channel_id=1, source_target_pairs={{0,1},{1,0},{2,3},{3,2},{4,5},{5,4},{6,7},{7,6},{8,9},{9,8},{10,11... | collective-permute-start | bytes 1658888 | tf_op jit(solution)/shard_map/source_fields/ppermute | solution.py:390
  56.7 4.6 %collective-permute-start.12 = (f32[4,3,48,240]{3,2,1,0:T(8,128)S(1)}, f32[4,3,48,240]{3,2,1,0:T(8,128)S(1)}, u32[]{:S(2)}, u32[]{:S(2)}) collective-permute-start(f32[4,3,48,240]{3,2,1,0:T(8,128)S(1)} %collective-permute-done.11.refs_10_.refs_8_), channel_id=1, source_target_pairs={{0,1},{1,0},{2,3},{3,2},{4,5},{5,4},{6,7},{7,6},{8,9},{9,8},{10,11... | collective-permute-start | bytes 1658888 | tf_op jit(solution)/shard_map/source_fields/ppermute | solution.py:390
  61.3 2.2 %collective-permute-start.18 = (f32[4,3,48,240]{3,2,1,0:T(8,128)S(1)}, f32[4,3,48,240]{3,2,1,0:T(8,128)S(1)}, u32[]{:S(2)}, u32[]{:S(2)}) collective-permute-start(f32[4,3,48,240]{3,2,1,0:T(8,128)S(1)} %collective-permute-done.17.refs_16_.refs_14_), channel_id=1, source_target_pairs={{0,1},{1,0},{2,3},{3,2},{4,5},{5,4},{6,7},{7,6},{8,9},{9,8},{10,11... | collective-permute-start | bytes 1658888 | tf_op jit(solution)/shard_map/source_fields/ppermute | solution.py:390
  63.4 1.1 collective-permute-start.15
  64.5 2.5 %collective-permute-start.20 = (f32[4,3,48,240]{3,2,1,0:T(8,128)S(1)}, f32[4,3,48,240]{3,2,1,0:T(8,128)}, u32[]{:S(2)}, u32[]{:S(2)}) collective-permute-start(f32[4,3,48,240]{3,2,1,0:T(8,128)S(1)} %collective-permute-done.19.refs_18_.refs_16_), channel_id=1, source_target_pairs={{0,1},{1,0},{2,3},{3,2},{4,5},{5,4},{6,7},{7,6},{8,9},{9,8},{10,11... | collective-permute-start | bytes 1658888 | tf_op jit(solution)/shard_map/source_fields/ppermute | solution.py:390
  69.2 26.7 %pair_terms.1 = (f32[2,2,3,48,240]{4,3,2,1,0:T(8,128)}, f32[2,2,3,48,240]{4,3,2,1,0:T(8,128)}, f32[2,3,48,240]{3,2,1,0:T(8,128)}, f32[2,3,48,240]{3,2,1,0:T(8,128)}, f32[2,2,3,48,240]{4,3,2,1,0:T(8,128)}) custom-call(s32[4]{0:T(128)} %pad_add_fusion.place.refs_0_, bf16[1248,768]{1,0:T(8,128)(2,1)} %constant.73.clone.refs_1_, f32[48,48,240]{2,1,0:T(8,128)} %refs_2_.1, ...), custom_call_target="tpu_custom_call" | custom-call | flops 1000 | bytes 1000 | tf_op jit(solution)/shard_map/pair_terms/pallas_call | solution.py:237
  95.9 2.2 %collective-permute-start.21 = (f32[2,2,3,48,240]{4,3,2,1,0:T(8,128)}, f32[2,2,3,48,240]{4,3,2,1,0:T(8,128)S(1)}, u32[]{:S(2)}, u32[]{:S(2)}) collective-permute-start(f32[2,2,3,48,240]{4,3,2,1,0:T(8,128)} %get-tuple-element.10), channel_id=1, source_target_pairs={{0,6},{2,0},{4,2},{6,4},{1,7},{3,1},{5,3},{7,5},{8,14},{10,8},{12,... | collective-permute-start | bytes 1658888 | tf_op jit(solution)/shard_map/sum_partials/ppermute | solution.py:390
  98.1 13.0 %collective-permute-done.21 = f32[2,2,3,48,240]{4,3,2,1,0:T(8,128)S(1)} collective-permute-done((f32[2,2,3,48,240]{4,3,2,1,0:T(8,128)}, f32[2,2,3,48,240]{4,3,2,1,0:T(8,128)S(1)}, u32[]{:S(2)}, u32[]{:S(2)}) %collective-permute-start.21) | collective-permute-done | bytes 552992 | tf_op jit(solution)/shard_map/sum_partials/ppermute | solution.py:390
  112.0 3.4 %collective-permute-start.24 = (f32[2,3,48,240]{3,2,1,0:T(8,128)S(1)}, f32[2,3,48,240]{3,2,1,0:T(8,128)S(1)}, u32[]{:S(2)}, u32[]{:S(2)}) collective-permute-start(f32[2,3,48,240]{3,2,1,0:T(8,128)S(1)} %fusion.1), channel_id=1, source_target_pairs={{0,6},{2,0},{4,2},{6,4},{1,7},{3,1},{5,3},{7,5},{8,14},{10,8},{12,... | collective-permute-start | bytes 829448 | tf_op jit(solution)/shard_map/sum_partials/ppermute | solution.py:390
  116.8 4.1 %collective-permute-done.24 = f32[2,3,48,240]{3,2,1,0:T(8,128)S(1)} collective-permute-done((f32[2,3,48,240]{3,2,1,0:T(8,128)S(1)}, f32[2,3,48,240]{3,2,1,0:T(8,128)S(1)}, u32[]{:S(2)}, u32[]{:S(2)}) %collective-permute-start.24) | collective-permute-done | bytes 276512 | tf_op jit(solution)/shard_map/sum_partials/ppermute | solution.py:390
  120.9 4.5 %collective-permute-done.23 = f32[2,3,48,240]{3,2,1,0:T(8,128)S(1)} collective-permute-done((f32[2,3,48,240]{3,2,1,0:T(8,128)S(1)}, f32[2,3,48,240]{3,2,1,0:T(8,128)S(1)}, u32[]{:S(2)}, u32[]{:S(2)}) %collective-permute-start.23) | collective-permute-done | bytes 276512 | tf_op jit(solution)/shard_map/sum_partials/ppermute | solution.py:390
  125.4 1.2 fusion.6
  126.7 2.1 %collective-permute-start.25 = (f32[2,3,48,240]{3,2,1,0:T(8,128)S(1)}, f32[2,3,48,240]{3,2,1,0:T(8,128)S(1)}, u32[]{:S(2)}, u32[]{:S(2)}) collective-permute-start(f32[2,3,48,240]{3,2,1,0:T(8,128)S(1)} %pad_maximum_fusion.4), channel_id=1, source_target_pairs={{0,1},{1,0},{2,3},{3,2},{4,5},{5,4},{6,7},{7,6},{8,9},{9,8},{10,11... | collective-permute-start | bytes 829448 | tf_op jit(solution)/shard_map/to_slabs/ppermute | solution.py:390
  128.7 1.2 collective-permute-done.25
  130.4 9.4 %collective-permute-start.27 = (f32[2,3,24,240]{3,2,1,0:T(8,128)S(1)}, f32[2,3,24,240]{3,2,1,0:T(8,128)S(1)}, u32[]{:S(2)}, u32[]{:S(2)}) collective-permute-start(f32[2,3,24,240]{3,2,1,0:T(8,128)S(1)} %fusion.8), channel_id=1, source_target_pairs={{0,16},{16,0},{1,17},{17,1},{2,18},{18,2},{3,19},{19,3},{4,20},{20... | collective-permute-start | bytes 414728 | tf_op jit(solution)/shard_map/to_slabs/ppermute | solution.py:390
  140.8 8.7 %collective-permute-done.27.straight = f32[2,3,24,240]{3,2,1,0:T(8,128)S(1)} collective-permute-done((f32[2,3,24,240]{3,2,1,0:T(8,128)S(1)}, f32[2,3,24,240]{3,2,1,0:T(8,128)S(1)}, u32[]{:S(2)}, u32[]{:S(2)}) %collective-permute-start.27) | collective-permute-done | bytes 138272 | tf_op jit(solution)/shard_map/to_slabs/ppermute | solution.py:390
  150.4 6.8 %margin_shares.1 = (f32[32,1,256]{2,1,0:T(1,128)}, f32[4,3,48,240]{3,2,1,0:T(8,128)}) custom-call(s32[4]{0:T(128)} %pad_add_fusion.place.refs_0_, f32[2,3,48,240]{3,2,1,0:T(8,128)} %pad_maximum_fusion.kept, f32[2,3,48,240]{3,2,1,0:T(8,128)} %copy-done.16, f32[2,3,24,240]{3,2,1,0:T(8,128)} %copy-done.18, f32[2,3,24,240]{3,2,1,0:T(8,128)} %copy-done.19, ...), custom_call_target="tpu_custom_call" | custom-call | flops 1000 | bytes 1000 | tf_op jit(solution)/shard_map/margin/margin_shares/pallas_call | solution.py:363
  157.2 12.1 %all_to_all.5 = f32[32,1,256]{2,1,0:T(1,128)S(1)} all-to-all(f32[32,1,256]{2,1,0:T(1,128)} %get-tuple-element.15), channel_id=1, replica_groups=mesh['z'=8,'xh'=2,'xl'=2,'y'=4,'core'=2] {'xh','xl','y','core'}, dimensions={0} | all-to-all | bytes 65536 | tf_op jit(solution)/shard_map/margin/all_to_all | solution.py:474
  (101 shorter events, 15.4 us)
Async XLA Ops:
  7.2 142.4 %all-gather.2.cloned.1.call-start = ((), (), s32[]{:S(2)}) async-start(), calls=%async_computation.1 | async-start | bytes 5308416 | tf_op jit(solution)/shard_map/all_orbitals/all_gather | solution.py:454
  8.8 4.5 %collective-permute-start = (f32[2,3,48,240]{3,2,1,0:T(8,128)S(1)}, f32[2,3,48,240]{3,2,1,0:T(8,128)S(1)}, u32[]{:S(2)}, u32[]{:S(2)}) collective-permute-start(f32[2,3,48,240]{3,2,1,0:T(8,128)S(1)} %pad_maximum_fusion.2), channel_id=1, source_target_pairs={{0,1},{1,0},{2,3},{3,2},{4,5},{5,4},{6,7},{7,6},{8,9},{9,8},{10,11... | collective-permute-start | bytes 829448 | tf_op jit(solution)/shard_map/target_slabs/ppermute | solution.py:390
  12.1 10.2 %collective-permute-start.3 = (f32[4,3,24,240]{3,2,1,0:T(8,128)S(1)}, f32[4,3,24,240]{3,2,1,0:T(8,128)S(1)}, u32[]{:S(2)}, u32[]{:S(2)}) collective-permute-start(f32[4,3,24,240]{3,2,1,0:T(8,128)S(1)} %constant_dynamic-slice_fusion.1), channel_id=1, source_target_pairs={{0,16},{16,0},{1,17},{17,1},{2,18},{18,2},{3,19},{19,3},{4,20},{20... | collective-permute-start | bytes 829448 | tf_op jit(solution)/shard_map/all_orbitals/ppermute | solution.py:390
  13.4 13.6 %collective-permute-start.1 = (f32[2,3,48,240]{3,2,1,0:T(8,128)S(1)}, f32[2,3,48,240]{3,2,1,0:T(8,128)S(1)}, u32[]{:S(2)}, u32[]{:S(2)}) collective-permute-start(f32[2,3,48,240]{3,2,1,0:T(8,128)S(1)} %pad_maximum_fusion.3), channel_id=1, source_target_pairs={{0,8},{8,0},{1,9},{9,1},{2,10},{10,2},{3,11},{11,3},{4,12},{12,4},... | collective-permute-start | bytes 829448 | tf_op jit(solution)/shard_map/target_slabs/ppermute | solution.py:390
  13.7 6.3 %collective-permute-start.2 = (f32[3,48,240]{2,1,0:T(8,128)S(1)}, f32[3,48,240]{2,1,0:T(8,128)S(1)}, u32[]{:S(2)}, u32[]{:S(2)}) collective-permute-start(f32[3,48,240]{2,1,0:T(8,128)S(1)} %get-tuple-element.23), channel_id=1, source_target_pairs={{0,4},{2,6},{4,0},{6,2},{1,5},{3,7},{5,1},{7,3},{8,12},{10,14},{12... | collective-permute-start | bytes 414728 | tf_op jit(solution)/shard_map/source_slabs/ppermute | solution.py:390
  16.6 14.5 %collective-permute-start.9 = (f32[3,48,240]{2,1,0:T(8,128)S(1)}, f32[3,48,240]{2,1,0:T(8,128)S(1)}, u32[]{:S(2)}, u32[]{:S(2)}) collective-permute-start(f32[3,48,240]{2,1,0:T(8,128)S(1)} %get-tuple-element.28), channel_id=1, source_target_pairs={{0,6},{2,0},{4,2},{6,4},{1,7},{3,1},{5,3},{7,5},{8,14},{10,8},{12,... | collective-permute-start | bytes 414728 | tf_op jit(solution)/shard_map/source_slabs/ppermute | solution.py:390
  17.4 13.8 %collective-permute-start.8 = (f32[3,48,240]{2,1,0:T(8,128)S(1)}, f32[3,48,240]{2,1,0:T(8,128)S(1)}, u32[]{:S(2)}, u32[]{:S(2)}) collective-permute-start(f32[3,48,240]{2,1,0:T(8,128)S(1)} %get-tuple-element.29), channel_id=1, source_target_pairs={{0,2},{2,4},{4,6},{6,0},{1,3},{3,5},{5,7},{7,1},{8,10},{10,12},{12... | collective-permute-start | bytes 414728 | tf_op jit(solution)/shard_map/source_slabs/ppermute | solution.py:390
  28.3 40.8 %copy-start.2 = (f32[2,2,3,48,240]{4,3,2,1,0:T(8,128)}, f32[2,2,3,48,240]{4,3,2,1,0:T(8,128)S(1)}, u32[]{:S(2)}) copy-start(f32[2,2,3,48,240]{4,3,2,1,0:T(8,128)S(1)} %fusion.refs_3_.refs_1_) | copy-start | bytes 1658884
  28.3 14.1 %collective-permute-start.6 = (f32[2,2,3,48,240]{4,3,2,1,0:T(8,128)S(1)}, f32[2,2,3,48,240]{4,3,2,1,0:T(8,128)S(1)}, u32[]{:S(2)}, u32[]{:S(2)}) collective-permute-start(f32[2,2,3,48,240]{4,3,2,1,0:T(8,128)S(1)} %fusion.refs_3_.refs_1_), channel_id=1, source_target_pairs={{0,6},{2,0},{4,2},{6,4},{1,7},{3,1},{5,3},{7,5},{8,14},{10,8},{12,... | collective-permute-start | bytes 1658888 | tf_op jit(solution)/shard_map/target_slabs/ppermute | solution.py:390
  31.2 37.9 %copy-start.1 = (f32[4,3,48,240]{3,2,1,0:T(8,128)}, f32[4,3,48,240]{3,2,1,0:T(8,128)S(1)}, u32[]{:S(2)}) copy-start(f32[4,3,48,240]{3,2,1,0:T(8,128)S(1)} %maximum_add_fusion.1.refs_8_.refs_6_) | copy-start | bytes 1658884
  31.2 17.6 %collective-permute-start.13 = (f32[4,3,48,240]{3,2,1,0:T(8,128)S(1)}, f32[4,3,48,240]{3,2,1,0:T(8,128)S(1)}, u32[]{:S(2)}, u32[]{:S(2)}) collective-permute-start(f32[4,3,48,240]{3,2,1,0:T(8,128)S(1)} %maximum_add_fusion.1.refs_8_.refs_6_), channel_id=1, source_target_pairs={{0,24},{8,16},{16,40},{24,32},{32,56},{40,48},{48,72},{56,64},{64,... | collective-permute-start | bytes 1658888 | tf_op jit(solution)/shard_map/source_fields/ppermute | solution.py:403
  31.9 18.1 %collective-permute-start.11 = (f32[4,3,48,240]{3,2,1,0:T(8,128)S(1)}, f32[4,3,48,240]{3,2,1,0:T(8,128)S(1)}, u32[]{:S(2)}, u32[]{:S(2)}) collective-permute-start(f32[4,3,48,240]{3,2,1,0:T(8,128)S(1)} %maximum_add_fusion.1.refs_8_.refs_6_), channel_id=1, source_target_pairs={{0,8},{8,0},{1,9},{9,1},{2,10},{10,2},{3,11},{11,3},{4,12},{12,4},... | collective-permute-start | bytes 1658888 | tf_op jit(solution)/shard_map/source_fields/ppermute | solution.py:390
  32.7 17.4 %collective-permute-start.4 = (f32[2,2,3,48,240]{4,3,2,1,0:T(8,128)S(1)}, f32[2,2,3,48,240]{4,3,2,1,0:T(8,128)S(1)}, u32[]{:S(2)}, u32[]{:S(2)}) collective-permute-start(f32[2,2,3,48,240]{4,3,2,1,0:T(8,128)S(1)} %fusion.refs_3_.refs_1_), channel_id=1, source_target_pairs={{0,2},{2,4},{4,6},{6,0},{1,3},{3,5},{5,7},{7,1},{8,10},{10,12},{12... | collective-permute-start | bytes 1658888 | tf_op jit(solution)/shard_map/target_slabs/ppermute | solution.py:390
  32.7 18.3 %collective-permute-start.17 = (f32[4,3,48,240]{3,2,1,0:T(8,128)S(1)}, f32[4,3,48,240]{3,2,1,0:T(8,128)S(1)}, u32[]{:S(2)}, u32[]{:S(2)}) collective-permute-start(f32[4,3,48,240]{3,2,1,0:T(8,128)S(1)} %maximum_add_fusion.1.refs_8_.refs_6_), channel_id=1, source_target_pairs={{0,32},{32,64},{64,96},{96,128},{128,160},{160,192},{192,224},{224... | collective-permute-start | bytes 1658888 | tf_op jit(solution)/shard_map/source_fields/ppermute | solution.py:390
  42.5 9.3 %collective-permute-start.10 = (f32[4,3,48,240]{3,2,1,0:T(8,128)S(1)}, f32[4,3,48,240]{3,2,1,0:T(8,128)S(1)}, u32[]{:S(2)}, u32[]{:S(2)}) collective-permute-start(f32[4,3,48,240]{3,2,1,0:T(8,128)S(1)} %maximum_add_fusion.1.refs_8_.refs_6_), channel_id=1, source_target_pairs={{0,1},{1,0},{2,3},{3,2},{4,5},{5,4},{6,7},{7,6},{8,9},{9,8},{10,11... | collective-permute-start | bytes 1658888 | tf_op jit(solution)/shard_map/source_fields/ppermute | solution.py:390
  48.8 14.6 %collective-permute-start.14 = (f32[4,3,48,240]{3,2,1,0:T(8,128)S(1)}, f32[4,3,48,240]{3,2,1,0:T(8,128)S(1)}, u32[]{:S(2)}, u32[]{:S(2)}) collective-permute-start(f32[4,3,48,240]{3,2,1,0:T(8,128)S(1)} %collective-permute-done.13.refs_14_.refs_12_), channel_id=1, source_target_pairs={{0,8},{8,0},{1,9},{9,1},{2,10},{10,2},{3,11},{11,3},{4,12},{12,4},... | collective-permute-start | bytes 1658888 | tf_op jit(solution)/shard_map/source_fields/ppermute | solution.py:390
  50.1 14.5 %collective-permute-start.19 = (f32[4,3,48,240]{3,2,1,0:T(8,128)S(1)}, f32[4,3,48,240]{3,2,1,0:T(8,128)S(1)}, u32[]{:S(2)}, u32[]{:S(2)}) collective-permute-start(f32[4,3,48,240]{3,2,1,0:T(8,128)S(1)} %collective-permute-done.11.refs_10_.refs_8_), channel_id=1, source_target_pairs={{0,32},{32,64},{64,96},{96,128},{128,160},{160,192},{192,224},{224... | collective-permute-start | bytes 1658888 | tf_op jit(solution)/shard_map/source_fields/ppermute | solution.py:390
  50.1 6.6 %collective-permute-start.7 = (f32[2,3,48,240]{3,2,1,0:T(8,128)S(1)}, f32[2,3,48,240]{3,2,1,0:T(8,128)S(1)}, u32[]{:S(2)}, u32[]{:S(2)}) collective-permute-start(f32[2,3,48,240]{3,2,1,0:T(8,128)S(1)} %slice_bitcast_fusion.2), channel_id=1, source_target_pairs={{0,6},{2,0},{4,2},{6,4},{1,7},{3,1},{5,3},{7,5},{8,14},{10,8},{12,... | collective-permute-start | bytes 829448 | tf_op jit(solution)/shard_map/target_slabs/ppermute | solution.py:390
  51.1 10.2 %collective-permute-start.5 = (f32[2,3,48,240]{3,2,1,0:T(8,128)S(1)}, f32[2,3,48,240]{3,2,1,0:T(8,128)}, u32[]{:S(2)}, u32[]{:S(2)}) collective-permute-start(f32[2,3,48,240]{3,2,1,0:T(8,128)S(1)} %slice_bitcast_fusion.3), channel_id=1, source_target_pairs={{0,2},{2,4},{4,6},{6,0},{1,3},{3,5},{5,7},{7,1},{8,10},{10,12},{12... | collective-permute-start | bytes 829448 | tf_op jit(solution)/shard_map/target_slabs/ppermute | solution.py:390
  51.8 15.2 %collective-permute-start.16 = (f32[4,3,48,240]{3,2,1,0:T(8,128)S(1)}, f32[4,3,48,240]{3,2,1,0:T(8,128)S(1)}, u32[]{:S(2)}, u32[]{:S(2)}) collective-permute-start(f32[4,3,48,240]{3,2,1,0:T(8,128)S(1)} %collective-permute-done.13.refs_14_.refs_12_), channel_id=1, source_target_pairs={{0,1},{1,0},{2,3},{3,2},{4,5},{5,4},{6,7},{7,6},{8,9},{9,8},{10,11... | collective-permute-start | bytes 1658888 | tf_op jit(solution)/shard_map/source_fields/ppermute | solution.py:390
  56.7 10.3 %collective-permute-start.12 = (f32[4,3,48,240]{3,2,1,0:T(8,128)S(1)}, f32[4,3,48,240]{3,2,1,0:T(8,128)S(1)}, u32[]{:S(2)}, u32[]{:S(2)}) collective-permute-start(f32[4,3,48,240]{3,2,1,0:T(8,128)S(1)} %collective-permute-done.11.refs_10_.refs_8_), channel_id=1, source_target_pairs={{0,1},{1,0},{2,3},{3,2},{4,5},{5,4},{6,7},{7,6},{8,9},{9,8},{10,11... | collective-permute-start | bytes 1658888 | tf_op jit(solution)/shard_map/source_fields/ppermute | solution.py:390
  61.3 5.8 %collective-permute-start.18 = (f32[4,3,48,240]{3,2,1,0:T(8,128)S(1)}, f32[4,3,48,240]{3,2,1,0:T(8,128)S(1)}, u32[]{:S(2)}, u32[]{:S(2)}) collective-permute-start(f32[4,3,48,240]{3,2,1,0:T(8,128)S(1)} %collective-permute-done.17.refs_16_.refs_14_), channel_id=1, source_target_pairs={{0,1},{1,0},{2,3},{3,2},{4,5},{5,4},{6,7},{7,6},{8,9},{9,8},{10,11... | collective-permute-start | bytes 1658888 | tf_op jit(solution)/shard_map/source_fields/ppermute | solution.py:390
  63.4 3.6 %collective-permute-start.15 = (f32[4,3,48,240]{3,2,1,0:T(8,128)S(1)}, f32[4,3,48,240]{3,2,1,0:T(8,128)S(1)}, u32[]{:S(2)}, u32[]{:S(2)}) collective-permute-start(f32[4,3,48,240]{3,2,1,0:T(8,128)S(1)} %collective-permute-done.14.refs_12_.refs_10_), channel_id=1, source_target_pairs={{0,1},{1,0},{2,3},{3,2},{4,5},{5,4},{6,7},{7,6},{8,9},{9,8},{10,11... | collective-permute-start | bytes 1658888 | tf_op jit(solution)/shard_map/source_fields/ppermute | solution.py:390
  64.5 4.6 %collective-permute-start.20 = (f32[4,3,48,240]{3,2,1,0:T(8,128)S(1)}, f32[4,3,48,240]{3,2,1,0:T(8,128)}, u32[]{:S(2)}, u32[]{:S(2)}) collective-permute-start(f32[4,3,48,240]{3,2,1,0:T(8,128)S(1)} %collective-permute-done.19.refs_18_.refs_16_), channel_id=1, source_target_pairs={{0,1},{1,0},{2,3},{3,2},{4,5},{5,4},{6,7},{7,6},{8,9},{9,8},{10,11... | collective-permute-start | bytes 1658888 | tf_op jit(solution)/shard_map/source_fields/ppermute | solution.py:390
  95.9 15.2 %collective-permute-start.21 = (f32[2,2,3,48,240]{4,3,2,1,0:T(8,128)}, f32[2,2,3,48,240]{4,3,2,1,0:T(8,128)S(1)}, u32[]{:S(2)}, u32[]{:S(2)}) collective-permute-start(f32[2,2,3,48,240]{4,3,2,1,0:T(8,128)} %get-tuple-element.10), channel_id=1, source_target_pairs={{0,6},{2,0},{4,2},{6,4},{1,7},{3,1},{5,3},{7,5},{8,14},{10,8},{12,... | collective-permute-start | bytes 1658888 | tf_op jit(solution)/shard_map/sum_partials/ppermute | solution.py:390
  98.1 17.4 %collective-permute-start.22 = (f32[2,2,3,48,240]{4,3,2,1,0:T(8,128)}, f32[2,2,3,48,240]{4,3,2,1,0:T(8,128)S(1)}, u32[]{:S(2)}, u32[]{:S(2)}) collective-permute-start(f32[2,2,3,48,240]{4,3,2,1,0:T(8,128)} %get-tuple-element.12), channel_id=1, source_target_pairs={{0,2},{2,4},{4,6},{6,0},{1,3},{3,5},{5,7},{7,1},{8,10},{10,12},{12... | collective-permute-start | bytes 1658888 | tf_op jit(solution)/shard_map/sum_partials/ppermute | solution.py:390
  112.0 8.9 %collective-permute-start.24 = (f32[2,3,48,240]{3,2,1,0:T(8,128)S(1)}, f32[2,3,48,240]{3,2,1,0:T(8,128)S(1)}, u32[]{:S(2)}, u32[]{:S(2)}) collective-permute-start(f32[2,3,48,240]{3,2,1,0:T(8,128)S(1)} %fusion.1), channel_id=1, source_target_pairs={{0,6},{2,0},{4,2},{6,4},{1,7},{3,1},{5,3},{7,5},{8,14},{10,8},{12,... | collective-permute-start | bytes 829448 | tf_op jit(solution)/shard_map/sum_partials/ppermute | solution.py:390
  116.5 9.0 %collective-permute-start.23 = (f32[2,3,48,240]{3,2,1,0:T(8,128)S(1)}, f32[2,3,48,240]{3,2,1,0:T(8,128)S(1)}, u32[]{:S(2)}, u32[]{:S(2)}) collective-permute-start(f32[2,3,48,240]{3,2,1,0:T(8,128)S(1)} %fusion.4), channel_id=1, source_target_pairs={{0,2},{2,4},{4,6},{6,0},{1,3},{3,5},{5,7},{7,1},{8,10},{10,12},{12... | collective-permute-start | bytes 829448 | tf_op jit(solution)/shard_map/sum_partials/ppermute | solution.py:390
  126.7 3.3 %collective-permute-start.25 = (f32[2,3,48,240]{3,2,1,0:T(8,128)S(1)}, f32[2,3,48,240]{3,2,1,0:T(8,128)S(1)}, u32[]{:S(2)}, u32[]{:S(2)}) collective-permute-start(f32[2,3,48,240]{3,2,1,0:T(8,128)S(1)} %pad_maximum_fusion.4), channel_id=1, source_target_pairs={{0,1},{1,0},{2,3},{3,2},{4,5},{5,4},{6,7},{7,6},{8,9},{9,8},{10,11... | collective-permute-start | bytes 829448 | tf_op jit(solution)/shard_map/to_slabs/ppermute | solution.py:390
  130.0 19.6 %collective-permute-start.26 = (f32[2,3,48,240]{3,2,1,0:T(8,128)S(1)}, f32[2,3,48,240]{3,2,1,0:T(8,128)S(1)}, u32[]{:S(2)}, u32[]{:S(2)}) collective-permute-start(f32[2,3,48,240]{3,2,1,0:T(8,128)S(1)} %pad_maximum_fusion.1), channel_id=1, source_target_pairs={{0,8},{8,0},{1,9},{9,1},{2,10},{10,2},{3,11},{11,3},{4,12},{12,4},... | collective-permute-start | bytes 829448 | tf_op jit(solution)/shard_map/to_slabs/ppermute | solution.py:390
  130.4 19.1 %collective-permute-start.27 = (f32[2,3,24,240]{3,2,1,0:T(8,128)S(1)}, f32[2,3,24,240]{3,2,1,0:T(8,128)S(1)}, u32[]{:S(2)}, u32[]{:S(2)}) collective-permute-start(f32[2,3,24,240]{3,2,1,0:T(8,128)S(1)} %fusion.8), channel_id=1, source_target_pairs={{0,16},{16,0},{1,17},{17,1},{2,18},{18,2},{3,19},{19,3},{4,20},{20... | collective-permute-start | bytes 414728 | tf_op jit(solution)/shard_map/to_slabs/ppermute | solution.py:390
  139.8 9.8 %collective-permute-start.28 = (f32[2,3,24,240]{3,2,1,0:T(8,128)S(1)}, f32[2,3,24,240]{3,2,1,0:T(8,128)S(1)}, u32[]{:S(2)}, u32[]{:S(2)}) collective-permute-start(f32[2,3,24,240]{3,2,1,0:T(8,128)S(1)} %fusion.7), channel_id=1, source_target_pairs={{0,24},{8,16},{16,8},{24,0},{1,25},{9,17},{17,9},{25,1},{2,26},{10... | collective-permute-start | bytes 414728 | tf_op jit(solution)/shard_map/to_slabs/ppermute | solution.py:403
  (18 other events, 146.8 us)
Sparse Core Ops, SparseCore 0:
  69.3 66.1 all-gather.1
